TPU v7x, 512 devices: a whole 4x8x8 slice. The times are simulated.
512 devices in a mesh: dp: 64 (over z, y), seq: 8 (over x, core).
Axes of the slice: x: 4, y: 8, z: 8, core: 2. Of those that a mesh axis runs over, the one named last changes fastest.
Arguments:
- queries: bfloat16 [512, 152, 4096], P(('dp', 'seq')), may hold values from -120 to 120
- candidate_keys: bfloat16 [512, 152, 1024], P(('dp', 'seq')), may hold values from -5 to 5
- candidate_values: bfloat16 [512, 152, 1024], P(('dp', 'seq')), may hold values from -6 to 6
- grad_output: bfloat16 [512, 152, 4096], P(('dp', 'seq')), may hold values from -24 to 24
- prefix_keys: bfloat16 [64, 56, 1024], P('dp', None, 'seq'), may hold values from -6 to 6
- prefix_values: bfloat16 [64, 56, 1024], P('dp', None, 'seq'), may hold values from -6 to 6
- query_index: int32 [512], replicated, may hold values from 0 to 63
- candidate_length: int32 [512], replicated, may hold values from 1 to 152, as said below
- prefix_length: int32 [64], replicated, may hold values from 1 to 56, as said below
Outputs:
- grad_queries: bfloat16 [512, 152, 4096], P(('dp', 'seq'))
- grad_candidate_keys: bfloat16 [512, 152, 1024], P(('dp', 'seq'))
- grad_candidate_values: bfloat16 [512, 152, 1024], P(('dp', 'seq'))
- grad_prefix_keys: float32 [64, 56, 1024], P('dp', None, 'seq')
- grad_prefix_values: float32 [64, 56, 1024], P('dp', None, 'seq')
Inputs may be any that keep to these rules, and one draw needn't show every extreme that they name: `candidate_length`: some candidate has all 152 tokens live. `prefix_length`: some query has all 56 prefix tokens live.
All inputs are finite; a program needn't handle non-finite values.
Results may differ from a plain program's by a relative error of at most 0.02.
Values may be sent and summed in bfloat16 or wider, within the bound.
No kernel may reach another device: no remote copies, remote signals or barrier semaphores. Data moves between devices by JAX's collectives and lax.ppermute only.
A program may use at most 64 MiB of HBM per device.

v0:
```python
import math

import jax
import jax.numpy as jnp
from jax import lax
from jax.sharding import PartitionSpec as P

HD = 128


def attend(
    queries, keys_in, values_in, grad_output, prefix_keys, prefix_values, lengths, prefix_lengths
):
    count, rows, width_q = queries.shape
    prefix_rows = prefix_keys.shape[1]
    kv_heads = keys_in.shape[2] // HD
    group = width_q // (kv_heads * HD)
    span = prefix_rows + rows
    scale = 1.0 / math.sqrt(HD)
    all_keys = jnp.concatenate([prefix_keys, keys_in], axis=1).reshape(count, span, kv_heads, HD)
    all_values = jnp.concatenate([prefix_values, values_in], axis=1).reshape(
        count, span, kv_heads, HD
    )
    query_heads = queries.reshape(count, rows, kv_heads, group, HD)
    position = jnp.arange(rows)[None, :, None]
    column = jnp.arange(span)[None, None, :]
    inside = column - prefix_rows
    allowed = jnp.where(
        column < prefix_rows,
        column < prefix_lengths[:, None, None],
        jnp.logical_and(inside <= position, inside < lengths[:, None, None]),
    )
    allowed = allowed[:, None, None]
    scores = (
        jnp.einsum("ctgrd,cugd->cgrtu", query_heads, all_keys, preferred_element_type=jnp.float32)
        * scale
    )
    scores = jnp.where(allowed, scores, -1e30)
    highest = jnp.max(scores, axis=-1, keepdims=True)
    expon = jnp.where(allowed, jnp.exp(scores - highest), 0.0)
    probs = expon / jnp.sum(expon, axis=-1, keepdims=True)
    probs_low = probs.astype(jnp.bfloat16)
    live = jnp.arange(rows)[None, :] < lengths[:, None]
    masked_grad = jnp.where(live[:, :, None], grad_output, jnp.zeros((), grad_output.dtype))
    grad_heads = masked_grad.reshape(count, rows, kv_heads, group, HD)
    attended = jnp.einsum(
        "cgrtu,cugd->ctgrd", probs_low, all_values, preferred_element_type=jnp.float32
    )
    delta = jnp.moveaxis(jnp.sum(grad_heads * attended, axis=-1), 1, 3)
    value_terms = jnp.einsum(
        "cgrtu,ctgrd->cugd", probs_low, grad_heads, preferred_element_type=jnp.float32
    )
    grad_probs = jnp.einsum(
        "ctgrd,cugd->cgrtu", grad_heads, all_values, preferred_element_type=jnp.float32
    )
    grad_scores = (probs * (grad_probs - delta[..., None]) * scale).astype(jnp.bfloat16)
    query_grads = jnp.einsum(
        "cgrtu,cugd->ctgrd", grad_scores, all_keys, preferred_element_type=jnp.float32
    )
    query_grads = query_grads.astype(jnp.bfloat16).reshape(count, rows, width_q)
    key_terms = jnp.einsum(
        "cgrtu,ctgrd->cugd", grad_scores, query_heads, preferred_element_type=jnp.float32
    )
    key_terms = key_terms.reshape(count, span, kv_heads * HD)
    value_terms = value_terms.reshape(count, span, kv_heads * HD)
    return (
        query_grads,
        key_terms[:, prefix_rows:].astype(jnp.bfloat16),
        value_terms[:, prefix_rows:].astype(jnp.bfloat16),
        key_terms[:, :prefix_rows],
        value_terms[:, :prefix_rows],
    )


def local(
    queries,
    candidate_keys,
    candidate_values,
    grad_output,
    prefix_keys,
    prefix_values,
    query_index,
    candidate_length,
    prefix_length,
):
    seq_count = lax.axis_size("seq")
    per_device = queries.shape[0]
    group_size = seq_count * per_device
    first = lax.axis_index("dp") * group_size
    group_query = lax.dynamic_slice_in_dim(query_index, first, group_size)
    group_length = lax.dynamic_slice_in_dim(candidate_length, first, group_size)
    total_queries = prefix_length.shape[0]
    lookup = group_query[:, None] == jnp.arange(total_queries)[None, :]
    group_prefix = jnp.sum(jnp.where(lookup, prefix_length[None, :], 0), axis=1)
    pieces = (
        lax.all_gather(prefix_keys, "dp", axis=0, tiled=True),
        lax.all_gather(prefix_values, "dp", axis=0, tiled=True),
    )
    count = pieces[0].shape[0]
    select = (group_query[:, None] == jnp.arange(count)[None, :]).astype(jnp.bfloat16)
    picked_keys = jnp.einsum("gq,qpf->gpf", select, pieces[0], preferred_element_type=jnp.float32)
    picked_values = jnp.einsum("gq,qpf->gpf", select, pieces[1], preferred_element_type=jnp.float32)
    picked_keys = picked_keys.astype(jnp.bfloat16)
    picked_values = picked_values.astype(jnp.bfloat16)
    head_queries, head_keys, head_values, head_grads = (
        lax.all_to_all(queries, "seq", split_axis=2, concat_axis=0, tiled=True),
        lax.all_to_all(candidate_keys, "seq", split_axis=2, concat_axis=0, tiled=True),
        lax.all_to_all(candidate_values, "seq", split_axis=2, concat_axis=0, tiled=True),
        lax.all_to_all(grad_output, "seq", split_axis=2, concat_axis=0, tiled=True),
    )
    query_grads, key_grads, value_grads, key_terms, value_terms = attend(
        head_queries,
        head_keys,
        head_values,
        head_grads,
        picked_keys,
        picked_values,
        group_length,
        group_prefix,
    )
    query_grads, key_grads, value_grads = (
        lax.all_to_all(query_grads, "seq", split_axis=0, concat_axis=2, tiled=True),
        lax.all_to_all(key_grads, "seq", split_axis=0, concat_axis=2, tiled=True),
        lax.all_to_all(value_grads, "seq", split_axis=0, concat_axis=2, tiled=True),
    )
    both_terms = jnp.concatenate([key_terms, value_terms], axis=2)
    row_ids = jnp.arange(prefix_keys.shape[0] * lax.axis_size("dp"))
    select = (row_ids[:, None] == group_query[None, :]).astype(jnp.float32)
    summed = lax.psum_scatter(
        jnp.einsum("qg,gpf->qpf", select, both_terms, precision=lax.Precision.HIGHEST),
        "dp",
        scatter_dimension=0,
        tiled=True,
    )
    width = prefix_keys.shape[2]
    return (query_grads, key_grads, value_grads, summed[:, :, :width], summed[:, :, width:])


def solution(mesh):
    in_specs = (
        P(("dp", "seq"), None, None),
        P(("dp", "seq"), None, None),
        P(("dp", "seq"), None, None),
        P(("dp", "seq"), None, None),
        P("dp", None, "seq"),
        P("dp", None, "seq"),
        P(),
        P(),
        P(),
    )
    out_specs = (
        P(("dp", "seq"), None, None),
        P(("dp", "seq"), None, None),
        P(("dp", "seq"), None, None),
        P("dp", None, "seq"),
        P("dp", None, "seq"),
    )
    return jax.shard_map(local, mesh=mesh, in_specs=in_specs, out_specs=out_specs, check_vma=False)
```

profile of v0, /device:TPU:2, one launch (start us, length us, event | category | flops | bytes accessed | tf_op | source)
XLA Modules:
  0.0 471.4 jit_solution(10987414764688925959)
XLA Ops:
  7.2 2.4 copy.86
  10.1 4.0 reduce.6
  16.0 9.4 %all-to-all-start = ((bf16[8,2,9728]{2,1,0:T(2,128)(2,1)}), bf16[8,2,9728]{2,1,0:T(2,128)(2,1)S(1)}, u32[]{:S(2)}, u32[]{:S(2)}) async-start(bf16[8,2,9728]{2,1,0:T(2,128)(2,1)} %reshape.223), calls=%async_computation | async-start | bytes 622592 | tf_op jit(solution)/shard_map/all_to_all | solution.py:107
  26.2 4.0 reduce.4
  32.0 5.3 %all-to-all-start.2 = ((bf16[8,2,9728]{2,1,0:T(2,128)(2,1)}), bf16[8,2,9728]{2,1,0:T(2,128)(2,1)S(1)}, u32[]{:S(2)}, u32[]{:S(2)}) async-start(bf16[8,2,9728]{2,1,0:T(2,128)(2,1)} %reshape.219), calls=%async_computation.2 | async-start | bytes 622592 | tf_op jit(solution)/shard_map/all_to_all | solution.py:108
  37.4 8.4 %copy.99 = bf16[1,152,4096]{1,0,2:T(2,128)(2,1)} copy(bf16[1,152,4096]{2,1,0:T(8,128)(2,1)S(1)} %copy-done.1) | data formatting | bytes 2490368 | tf_op args[3]
  45.7 23.6 %reduce.3 = bf16[4096,152]{1,0:T(8,128)(2,1)S(1)} reduce(bf16[4096,1,152]{2,1,0:T(2,128)(2,1)} %bitcast.165, bf16[]{:T(256)} %broadcast.154), dimensions={1}, to_apply=%bitcast.144.reduce_sub_computation | reduce | bytes 2490370
  69.4 5.4 %reshape.217 = bf16[8,2,38912]{2,1,0:T(2,128)(2,1)} reshape(bf16[4096,152]{1,0:T(8,128)(2,1)S(1)} %reduce.3) | data formatting | bytes 2490368
  76.3 4.8 %all-to-all-start.3 = ((bf16[8,2,38912]{2,1,0:T(2,128)(2,1)}), bf16[8,2,38912]{2,1,0:T(2,128)(2,1)S(1)}, u32[]{:S(2)}, u32[]{:S(2)}) async-start(bf16[8,2,38912]{2,1,0:T(2,128)(2,1)} %reshape.217), calls=%async_computation.3 | async-start | bytes 2490368 | tf_op jit(solution)/shard_map/all_to_all | solution.py:109
  82.0 8.3 %copy.90 = bf16[1,152,4096]{1,0,2:T(2,128)(2,1)} copy(bf16[1,152,4096]{2,1,0:T(8,128)(2,1)S(1)} %copy-done.2) | data formatting | bytes 2490368 | tf_op args[0]
  90.3 23.6 %reduce.5 = bf16[4096,152]{1,0:T(8,128)(2,1)S(1)} reduce(bf16[4096,1,152]{2,1,0:T(2,128)(2,1)} %bitcast.162, bf16[]{:T(256)} %broadcast.154), dimensions={1}, to_apply=%bitcast.148.reduce_sub_computation | reduce | bytes 2490370
  114.0 5.4 %reshape.221 = bf16[8,2,38912]{2,1,0:T(2,128)(2,1)} reshape(bf16[4096,152]{1,0:T(8,128)(2,1)S(1)} %reduce.5) | data formatting | bytes 2490368
  119.4 53.2 %all_gather.6 = bf16[64,56,128]{2,1,0:T(8,128)(2,1)S(1)} all-gather(bf16[1,56,128]{2,1,0:T(8,128)(2,1)S(1)} %copy-done.15), channel_id=1, replica_groups=mesh['dp'=64,'seq'=8] {'dp'}, dimensions={0}, use_global_device_ids=true | all-gather | bytes 931840 | tf_op jit(solution)/shard_map/all_gather | solution.py:96
  172.6 48.5 %all_gather.7 = bf16[64,56,128]{2,1,0:T(8,128)(2,1)S(1)} all-gather(bf16[1,56,128]{2,1,0:T(8,128)(2,1)S(1)} %copy-done.16), channel_id=1, replica_groups=mesh['dp'=64,'seq'=8] {'dp'}, dimensions={0}, use_global_device_ids=true | all-gather | bytes 931840 | tf_op jit(solution)/shard_map/all_gather | solution.py:97
  221.7 4.8 %all-to-all-start.1 = ((bf16[8,2,38912]{2,1,0:T(2,128)(2,1)}), bf16[8,2,38912]{2,1,0:T(2,128)(2,1)}, u32[]{:S(2)}, u32[]{:S(2)}) async-start(bf16[8,2,38912]{2,1,0:T(2,128)(2,1)} %reshape.221), calls=%async_computation.1 | async-start | bytes 2490368 | tf_op jit(solution)/shard_map/all_to_all | solution.py:106
  234.1 7.9 %reshape.218 = bf16[4096,1,152]{2,1,0:T(2,128)(2,1)} reshape(bf16[8,2,38912]{2,1,0:T(2,128)(2,1)S(1)} %all-to-all-done.3) | data formatting | bytes 2490368
  241.9 9.6 %copy.100 = bf16[1,152,4096]{2,1,0:T(8,128)(2,1)S(1)} copy(bf16[1,152,4096]{1,0,2:T(2,128)(2,1)} %bitcast.163) | data formatting | bytes 2490368 | tf_op jit(solution)/shard_map/all_to_all | solution.py:109
  253.7 8.9 %reshape.222 = bf16[4096,1,152]{2,1,0:T(2,128)(2,1)} reshape(bf16[8,2,38912]{2,1,0:T(2,128)(2,1)} %all-to-all-done.1) | data formatting | bytes 2490368
  262.5 9.6 %copy.91 = bf16[1,152,4096]{2,1,0:T(8,128)(2,1)S(1)} copy(bf16[1,152,4096]{1,0,2:T(2,128)(2,1)} %bitcast.164) | data formatting | bytes 2490368 | tf_op jit(solution)/shard_map/all_to_all | solution.py:106
  277.8 2.4 fusion.5
  280.2 4.4 fusion.14
  284.7 3.4 fusion.7
  288.1 2.8 fusion.6
  294.0 4.0 copy.112
  299.8 4.8 %all-to-all-start.5 = ((bf16[8,152,128]{2,1,0:T(8,128)(2,1)}), bf16[8,152,128]{2,1,0:T(8,128)(2,1)S(1)}, u32[]{:S(2)}, u32[]{:S(2)}) async-start(bf16[8,152,128]{2,1,0:T(8,128)(2,1)} %slice.33), calls=%async_computation.5 | async-start | bytes 622592 | tf_op jit(solution)/shard_map/all_to_all | solution.py:123
  306.5 4.8 %all-to-all-done.5 = bf16[8,152,128]{2,1,0:T(8,128)(2,1)S(1)} async-done(((bf16[8,152,128]{2,1,0:T(8,128)(2,1)}), bf16[8,152,128]{2,1,0:T(8,128)(2,1)S(1)}, u32[]{:S(2)}, u32[]{:S(2)}) %all-to-all-start.5) | async-done | bytes 311328 | tf_op jit(solution)/shard_map/all_to_all | solution.py:123
  311.3 4.8 %all-to-all-start.6 = ((bf16[8,152,128]{2,1,0:T(8,128)(2,1)}), bf16[8,152,128]{2,1,0:T(8,128)(2,1)S(1)}, u32[]{:S(2)}, u32[]{:S(2)}) async-start(bf16[8,152,128]{2,1,0:T(8,128)(2,1)} %slice.32), calls=%async_computation.6 | async-start | bytes 622592 | tf_op jit(solution)/shard_map/all_to_all | solution.py:124
  318.7 4.0 all-to-all-done.6
  322.7 4.9 %all-to-all-start.4 = ((bf16[8,152,512]{2,1,0:T(8,128)(2,1)}), bf16[8,152,512]{2,1,0:T(8,128)(2,1)S(1)}, u32[]{:S(2)}, u32[]{:S(2)}) async-start(bf16[8,152,512]{2,1,0:T(8,128)(2,1)} %reshape.203), calls=%async_computation.4 | async-start | bytes 2490368 | tf_op jit(solution)/shard_map/all_to_all | solution.py:122
  330.4 13.9 %all-to-all-done.4 = bf16[8,152,512]{2,1,0:T(8,128)(2,1)S(1)} async-done(((bf16[8,152,512]{2,1,0:T(8,128)(2,1)}), bf16[8,152,512]{2,1,0:T(8,128)(2,1)S(1)}, u32[]{:S(2)}, u32[]{:S(2)}) %all-to-all-start.4) | async-done | bytes 1245216 | tf_op jit(solution)/shard_map/all_to_all | solution.py:122
  345.4 116.9 %all-reduce.3.cloned.1.call-done = f32[64,56,256]{2,1,0:T(8,128)} async-done(((f32[64,56,256]{2,1,0:T(8,128)}), f32[64,56,256]{2,1,0:T(8,128)}) %all-reduce.3.cloned.1.call-update) | async-done | bytes 3670032
  462.3 2.0 constant_dynamic-slice_fusion.1
  (88 shorter events, 36.5 us)
Async XLA Ops:
  7.2 18.2 %copy-start.12 = (bf16[1,152,1024]{2,1,0:T(8,128)(2,1)S(1)}, bf16[1,152,1024]{2,1,0:T(8,128)(2,1)}, u32[]{:S(2)}) copy-start(bf16[1,152,1024]{2,1,0:T(8,128)(2,1)} %param.11) | copy-start | bytes 933892
  16.0 21.4 %copy-start.1 = (bf16[1,152,4096]{2,1,0:T(8,128)(2,1)S(1)}, bf16[1,152,4096]{2,1,0:T(8,128)(2,1)}, u32[]{:S(2)}) copy-start(bf16[1,152,4096]{2,1,0:T(8,128)(2,1)} %param.12) | copy-start | bytes 3735556
  16.0 16.1 %all-to-all-start = ((bf16[8,2,9728]{2,1,0:T(2,128)(2,1)}), bf16[8,2,9728]{2,1,0:T(2,128)(2,1)S(1)}, u32[]{:S(2)}, u32[]{:S(2)}) async-start(bf16[8,2,9728]{2,1,0:T(2,128)(2,1)} %reshape.223), calls=%async_computation | async-start | bytes 622592 | tf_op jit(solution)/shard_map/all_to_all | solution.py:107
  32.0 13.7 %copy-start.5 = (bf16[8,2,9728]{2,1,0:T(2,128)(2,1)}, bf16[8,2,9728]{2,1,0:T(2,128)(2,1)S(1)}, u32[]{:S(2)}) copy-start(bf16[8,2,9728]{2,1,0:T(2,128)(2,1)S(1)} %all-to-all-done) | copy-start | bytes 933892
  32.0 43.6 %all-to-all-start.2 = ((bf16[8,2,9728]{2,1,0:T(2,128)(2,1)}), bf16[8,2,9728]{2,1,0:T(2,128)(2,1)S(1)}, u32[]{:S(2)}, u32[]{:S(2)}) async-start(bf16[8,2,9728]{2,1,0:T(2,128)(2,1)} %reshape.219), calls=%async_computation.2 | async-start | bytes 622592 | tf_op jit(solution)/shard_map/all_to_all | solution.py:108
  74.8 7.2 %copy-start.2 = (bf16[1,152,4096]{2,1,0:T(8,128)(2,1)S(1)}, bf16[1,152,4096]{2,1,0:T(8,128)(2,1)}, u32[]{:S(2)}) copy-start(bf16[1,152,4096]{2,1,0:T(8,128)(2,1)} %param.9) | copy-start | bytes 3735556
  75.6 0.7 copy-start.7
  76.3 145.3 %all-to-all-start.3 = ((bf16[8,2,38912]{2,1,0:T(2,128)(2,1)}), bf16[8,2,38912]{2,1,0:T(2,128)(2,1)S(1)}, u32[]{:S(2)}, u32[]{:S(2)}) async-start(bf16[8,2,38912]{2,1,0:T(2,128)(2,1)} %reshape.217), calls=%async_computation.3 | async-start | bytes 2490368 | tf_op jit(solution)/shard_map/all_to_all | solution.py:109
  113.9 5.4 %copy-start.15 = (bf16[1,56,128]{2,1,0:T(8,128)(2,1)S(1)}, bf16[1,56,128]{2,1,0:T(8,128)(2,1)}, u32[]{:S(2)}) copy-start(bf16[1,56,128]{2,1,0:T(8,128)(2,1)} %param.13) | copy-start | bytes 43012
  113.9 58.6 %copy-start.16 = (bf16[1,56,128]{2,1,0:T(8,128)(2,1)S(1)}, bf16[1,56,128]{2,1,0:T(8,128)(2,1)}, u32[]{:S(2)}) copy-start(bf16[1,56,128]{2,1,0:T(8,128)(2,1)} %param.14) | copy-start | bytes 43012
  221.1 6.3 %copy-start.17 = (s32[64]{0:T(128)S(1)}, s32[64]{0:T(128)}, u32[]{:S(2)}) copy-start(s32[64]{0:T(128)} %param.17) | copy-start | bytes 772
  221.1 7.5 %copy-start.6 = (bf16[8,2,9728]{2,1,0:T(2,128)(2,1)S(1)}, bf16[8,2,9728]{2,1,0:T(2,128)(2,1)}, u32[]{:S(2)}) copy-start(bf16[8,2,9728]{2,1,0:T(2,128)(2,1)} %copy-done.5) | copy-start | bytes 933892
  221.7 32.0 %all-to-all-start.1 = ((bf16[8,2,38912]{2,1,0:T(2,128)(2,1)}), bf16[8,2,38912]{2,1,0:T(2,128)(2,1)}, u32[]{:S(2)}, u32[]{:S(2)}) async-start(bf16[8,2,38912]{2,1,0:T(2,128)(2,1)} %reshape.221), calls=%async_computation.1 | async-start | bytes 2490368 | tf_op jit(solution)/shard_map/all_to_all | solution.py:106
  226.5 4.8 %copy-start.8 = (bf16[8,2,9728]{2,1,0:T(2,128)(2,1)S(1)}, bf16[8,2,9728]{2,1,0:T(2,128)(2,1)}, u32[]{:S(2)}) copy-start(bf16[8,2,9728]{2,1,0:T(2,128)(2,1)} %copy-done.7) | copy-start | bytes 933892
  226.5 235.8 %all-reduce.3.cloned.1.call-start = ((), (), s32[]{:S(2)}) async-start(), calls=%async_computation.7 | async-start | bytes 7340032
  272.7 3.2 copy-start
  272.7 3.2 copy-start.9
  274.0 2.0 copy-start.4
  280.2 4.4 copy-start.3
  280.2 4.4 copy-start.13
  280.2 4.4 copy-start.14
  284.6 7.6 %copy-start.10 = (f32[8,208,128]{2,1,0:T(8,128)}, f32[8,208,128]{2,1,0:T(8,128)S(1)}, u32[]{:S(2)}) copy-start(f32[8,208,128]{2,1,0:T(8,128)S(1)} %fusion.14) | copy-start | bytes 2555908
  292.2 1.8 copy-start.11
  299.8 11.4 %all-to-all-start.5 = ((bf16[8,152,128]{2,1,0:T(8,128)(2,1)}), bf16[8,152,128]{2,1,0:T(8,128)(2,1)S(1)}, u32[]{:S(2)}, u32[]{:S(2)}) async-start(bf16[8,152,128]{2,1,0:T(8,128)(2,1)} %slice.33), calls=%async_computation.5 | async-start | bytes 622592 | tf_op jit(solution)/shard_map/all_to_all | solution.py:123
  311.3 11.4 %all-to-all-start.6 = ((bf16[8,152,128]{2,1,0:T(8,128)(2,1)}), bf16[8,152,128]{2,1,0:T(8,128)(2,1)S(1)}, u32[]{:S(2)}, u32[]{:S(2)}) async-start(bf16[8,152,128]{2,1,0:T(8,128)(2,1)} %slice.32), calls=%async_computation.6 | async-start | bytes 622592 | tf_op jit(solution)/shard_map/all_to_all | solution.py:124
  322.7 21.6 %all-to-all-start.4 = ((bf16[8,152,512]{2,1,0:T(8,128)(2,1)}), bf16[8,152,512]{2,1,0:T(8,128)(2,1)S(1)}, u32[]{:S(2)}, u32[]{:S(2)}) async-start(bf16[8,152,512]{2,1,0:T(8,128)(2,1)} %reshape.203), calls=%async_computation.4 | async-start | bytes 2490368 | tf_op jit(solution)/shard_map/all_to_all | solution.py:122
Sparse Core Ops, SparseCore 0:
  298.1 164.1 all-reduce.2
where the time goes:
time: 480 us; the launch traced here: 471 us
  waiting for transfers between devices  140 us (29%)
  blocking collectives  102 us (21%)
  local copies, waits for them, and re-layouts  98.6 us (21%)
  other arithmetic  61 us (13%)
  starting transfers between devices  39 us (8%)
  matrix products  16.8 us (4%)
  between operations  14.7 us (3%)
    unnamed x2, waiting for transfers between devices  117 us
    unnamed x54, local copies, waits for them, and re-layouts  58.2 us
    unnamed x4, other arithmetic  55.3 us
    all_gather x1, blocking collectives, local(): lax.all_gather(prefix_keys, 'dp', axis=0, tiled=True)  53.2 us
    all_gather x1, blocking collectives, local(): lax.all_gather(prefix_values, 'dp', axis=0, tiled=True)  48.5 us
    all_to_all x1, waiting for transfers between devices, local(): lax.all_to_all(query_grads, 'seq', split_axis=0, concat_axis=2, tiled=True)  13.9 us
    all_to_all x4, local copies, waits for them, and re-layouts, local(): lax.all_to_all(grad_output, 'seq', split_axis=2, concat_axis=0, tiled=True)  11.2 us
    all_to_all x2, local copies, waits for them, and re-layouts, local(): lax.all_to_all(queries, 'seq', split_axis=2, concat_axis=0, tiled=True)  9.67 us
  transfers between devices with their start and end apart: 8, of which 4 were waited for; matrix products, arithmetic and copies ran while one was open for 26% of the time, Pallas kernels for 0%

commit v1 on v0

v1 whole, which is shorter than its diff:
```python
import functools
import math

import jax
import jax.numpy as jnp
from jax import lax
from jax.experimental import pallas as pl
from jax.experimental.pallas import tpu as pltpu
from jax.sharding import Mesh, PartitionSpec as P

HD = 128
PAD = 16
NEG = -1e30
VMEM = 48 * 1024 * 1024


def stack_heads(ref, out, rows, group, stride):
    for h in range(group):
        out[pl.ds(h * stride, rows), :] = ref[0, :, h * HD : (h + 1) * HD]


def dot_nt(a, b):
    return lax.dot_general(a, b, (((1,), (1,)), ((), ())), preferred_element_type=jnp.float32)


def dot_nn(a, b):
    return lax.dot_general(a, b, (((1,), (0,)), ((), ())), preferred_element_type=jnp.float32)


def dot_tn(a, b):
    return lax.dot_general(a, b, (((0,), (0,)), ((), ())), preferred_element_type=jnp.float32)


def own_bias(bias, length, rows, group, stride):
    inside = lax.broadcasted_iota(jnp.int32, (rows, stride), 0)
    row = lax.broadcasted_iota(jnp.int32, (rows, stride), 1)
    tile = jnp.where(jnp.logical_and(inside <= row, inside < length), 0.0, NEG)
    bias[...] = jnp.concatenate([tile] * group, axis=1)


def prologue(q4, g4):
    q4[...] = jnp.zeros_like(q4)
    g4[...] = jnp.zeros_like(g4)


def own_stats(dims, meta, q, g, k, v, stats, q4, g4, bias):
    rows, group, stride, factor, _ = dims

    @pl.when(pl.program_id(0) == 0)
    def _():
        prologue(q4, g4)
        own_bias(bias, meta[0], rows, group, stride)

    stack_heads(q, q4, rows, group, stride)
    stack_heads(g, g4, rows, group, stride)
    scores = dot_nt(k[0], q4[...]) * factor + bias[...]
    highest = jnp.max(scores, axis=0, keepdims=True)
    expon = jnp.exp2(scores - highest)
    grad_probs = dot_nt(v[0], g4[...])
    stats[0, 0:1, :] = highest
    stats[0, 1:2, :] = jnp.sum(expon, axis=0, keepdims=True)
    stats[0, 2:3, :] = jnp.sum(expon * grad_probs, axis=0, keepdims=True)


def live_lanes(length, group, stride):
    row = lax.broadcasted_iota(jnp.int32, (1, stride), 1)
    live = jnp.where(row < length, 1.0, 0.0)
    return jnp.concatenate([live] * group, axis=1)


def prefix_bias(prefix_length, prefix_rows, width):
    column = lax.broadcasted_iota(jnp.int32, (prefix_rows, width), 0)
    return jnp.where(column < prefix_length, 0.0, NEG)


def prefix_terms(dims, meta, q, g, stats, pair, total, terms, q4, g4):
    rows, group, stride, factor, scale = dims
    prefix_rows = pair.shape[1]

    @pl.when(pl.program_id(0) == 0)
    def _():
        prologue(q4, g4)

    stack_heads(q, q4, rows, group, stride)
    stack_heads(g, g4, rows, group, stride)
    keys = pair[0, :, 0:HD]
    values = pair[0, :, HD : 2 * HD]
    scores = dot_nt(keys, q4[...]) * factor + prefix_bias(meta[1], prefix_rows, group * stride)
    own_high = stats[0, 0:1, :]
    highest = jnp.maximum(own_high, jnp.max(scores, axis=0, keepdims=True))
    expon = jnp.exp2(scores - highest)
    fade = jnp.exp2(own_high - highest)
    weight = fade * stats[0, 1:2, :] + jnp.sum(expon, axis=0, keepdims=True)
    inverse = live_lanes(meta[0], group, stride) / weight
    grad_probs = dot_nt(values, g4[...])
    delta = fade * stats[0, 2:3, :] + jnp.sum(expon * grad_probs, axis=0, keepdims=True)
    delta = delta * inverse
    probs = expon * inverse
    grad_scores = (probs * (grad_probs - delta) * scale).astype(jnp.bfloat16)
    total[0, 0:1, :] = highest
    total[0, 1:2, :] = inverse
    total[0, 2:3, :] = delta
    key_terms = dot_nn(grad_scores, q4[...])
    value_terms = dot_nn(probs.astype(jnp.bfloat16), g4[...])
    for side in range(terms.shape[0]):
        mine = meta[2] == side
        terms[side, 0, :, 0:HD] = jnp.where(mine, key_terms, 0.0).astype(jnp.bfloat16)
        terms[side, 0, :, HD : 2 * HD] = jnp.where(mine, value_terms, 0.0).astype(jnp.bfloat16)


def own_grads(dims, meta, q, g, k, v, total, pair, dq, dk, dv, q4, g4, bias):
    rows, group, stride, factor, scale = dims
    prefix_rows = pair.shape[1]

    @pl.when(pl.program_id(0) == 0)
    def _():
        prologue(q4, g4)
        own_bias(bias, meta[0], rows, group, stride)

    stack_heads(q, q4, rows, group, stride)
    stack_heads(g, g4, rows, group, stride)
    highest = total[0, 0:1, :]
    inverse = total[0, 1:2, :]
    delta = total[0, 2:3, :]

    def one(keys, values, mask):
        scores = dot_nt(keys, q4[...]) * factor + mask
        probs = jnp.exp2(scores - highest) * inverse
        grad_probs = dot_nt(values, g4[...])
        return probs, (probs * (grad_probs - delta) * scale).astype(jnp.bfloat16)

    keys = pair[0, :, 0:HD]
    values = pair[0, :, HD : 2 * HD]
    _, prefix_scores = one(keys, values, prefix_bias(meta[1], prefix_rows, group * stride))
    probs, grad_scores = one(k[0], v[0], bias[...])
    dv[0] = dot_nn(probs.astype(jnp.bfloat16), g4[...]).astype(jnp.bfloat16)
    dk[0] = dot_nn(grad_scores, q4[...]).astype(jnp.bfloat16)
    for h in range(group):
        lanes = slice(h * stride, (h + 1) * stride)
        rows_q = dot_tn(grad_scores[:, lanes], k[0]) + dot_tn(prefix_scores[:, lanes], keys)
        dq[0, :, h * HD : (h + 1) * HD] = rows_q[:rows].astype(jnp.bfloat16)


def pick_rows(index, source, out, sems):
    copies = [
        pltpu.make_async_copy(source.at[index[i]], out.at[i], sems.at[i])
        for i in range(out.shape[0])
    ]
    for copy in copies:
        copy.start()
    for copy in copies:
        copy.wait()


def add_rows(index, source, out, acc):
    acc[...] = jnp.zeros_like(acc)
    for i in range(source.shape[0]):
        at = index[i]
        acc[at] = acc[at] + source[i].astype(jnp.float32)
    out[...] = acc[...].astype(jnp.bfloat16)


def sum_rows(source, keys, values):
    total = source[0].astype(jnp.float32)
    for i in range(1, source.shape[0]):
        total = total + source[i].astype(jnp.float32)
    keys[0] = total[:, 0:HD]
    values[0] = total[:, HD : 2 * HD]


PARAMS = pltpu.CompilerParams(vmem_limit_bytes=VMEM)


def cost(flops, nbytes):
    return pl.CostEstimate(flops=flops, bytes_accessed=nbytes, transcendentals=flops // 256)


def local(
    queries,
    candidate_keys,
    candidate_values,
    grad_output,
    prefix_keys,
    prefix_values,
    query_index,
    candidate_length,
    prefix_length,
):
    far, near, seq = ("zh", "y"), ("zl", "seq"), "seq"
    rows, width_q = queries.shape[1:]
    kv_heads = candidate_keys.shape[2] // HD
    group = width_q // (kv_heads * HD)
    prefix_rows = prefix_keys.shape[1]
    stride = -(-rows // PAD) * PAD
    width = group * stride
    scale = 1.0 / math.sqrt(HD)
    dims = (rows, group, stride, scale * math.log2(math.e), scale)
    size_l, size_y, size_s = (lax.axis_size(a) for a in ("zl", "y", seq))
    size_h = lax.axis_size("zh")
    n_far, n_near = size_h * size_y, size_l * size_s
    zh, zl, y, s = (lax.axis_index(a) for a in ("zh", "zl", "y", seq))

    def place(query):
        z, owner_y = query // size_y, query % size_y
        return (z // size_l) * size_y + owner_y, z % size_l

    side = jnp.arange(size_l, dtype=jnp.int32)
    first = ((zh * size_l + side) * size_y + y) * size_s
    members = (first[:, None] + jnp.arange(size_s, dtype=jnp.int32)[None, :]).reshape(-1)
    member_far, member_zl = place(query_index[members])
    mine = ((zh * size_l + zl) * size_y + y) * size_s + s
    query = query_index[mine]
    _, query_zl = place(query)
    meta = jnp.stack([candidate_length[mine], prefix_length[query], query_zl]).astype(jnp.int32)

    smem = pl.BlockSpec(memory_space=pltpu.SMEM)
    any_space = pl.BlockSpec(memory_space=pl.ANY)
    vmem = pl.BlockSpec(memory_space=pltpu.VMEM)
    heads_q = pl.BlockSpec((1, rows, group * HD), lambda i, m: (0, 0, i))
    heads_k = pl.BlockSpec((1, rows, HD), lambda i, m: (0, 0, i))
    lanes = pl.BlockSpec((1, 8, width), lambda i, m: (i, 0, 0))
    picked = pl.BlockSpec(
        (1, prefix_rows, 2 * HD), lambda i, m: (m[2] * kv_heads + i, 0, 0)
    )
    packed = pltpu.VMEM((width, HD), jnp.bfloat16)
    bias = pltpu.VMEM((rows, width), jnp.float32)
    lane_shape = jax.ShapeDtypeStruct((kv_heads, 8, width), jnp.float32)
    big = kv_heads * width * rows * HD * 2

    own_pair = jnp.concatenate([prefix_keys[0], prefix_values[0]], axis=1)
    everyone = jnp.broadcast_to(own_pair[None], (n_far,) + own_pair.shape)
    held = lax.all_to_all(everyone, far, 0, 0, tiled=True)
    stats = pl.pallas_call(
        functools.partial(own_stats, dims),
        grid_spec=pltpu.PrefetchScalarGridSpec(
            num_scalar_prefetch=1,
            grid=(kv_heads,),
            in_specs=[heads_q, heads_q, heads_k, heads_k],
            out_specs=lanes,
            scratch_shapes=[packed, packed, bias],
        ),
        out_shape=lane_shape,
        compiler_params=PARAMS,
        cost_estimate=cost(2 * big, 3 << 20),
        name="own_stats",
    )(meta, queries, grad_output, candidate_keys, candidate_values)
    chosen = pl.pallas_call(
        pick_rows,
        in_specs=[smem, any_space],
        out_specs=any_space,
        out_shape=jax.ShapeDtypeStruct((n_near,) + own_pair.shape, jnp.bfloat16),
        scratch_shapes=[pltpu.SemaphoreType.DMA((n_near,))],
        compiler_params=PARAMS,
        name="pick_rows",
    )(member_far, held)
    pairs = lax.all_to_all(chosen, near, 0, 0, tiled=True)

    total, terms = pl.pallas_call(
        functools.partial(prefix_terms, dims),
        grid_spec=pltpu.PrefetchScalarGridSpec(
            num_scalar_prefetch=1,
            grid=(kv_heads,),
            in_specs=[heads_q, heads_q, lanes, picked],
            out_specs=[
                lanes,
                pl.BlockSpec((size_l, 1, prefix_rows, 2 * HD), lambda i, m: (0, i, 0, 0)),
            ],
            scratch_shapes=[packed, packed],
        ),
        out_shape=[
            lane_shape,
            jax.ShapeDtypeStruct((size_l, kv_heads, prefix_rows, 2 * HD), jnp.bfloat16),
        ],
        compiler_params=PARAMS,
        cost_estimate=cost(2 * big, 3 << 20),
        name="prefix_terms",
    )(meta, queries, grad_output, stats, pairs)

    returned = lax.all_to_all(
        terms.reshape(n_near, prefix_rows, 2 * HD), near, 0, 0, tiled=True
    )
    summed = pl.pallas_call(
        add_rows,
        in_specs=[smem, vmem],
        out_specs=vmem,
        out_shape=jax.ShapeDtypeStruct((n_far, prefix_rows, 2 * HD), jnp.bfloat16),
        scratch_shapes=[pltpu.VMEM((n_far, prefix_rows, 2 * HD), jnp.float32)],
        compiler_params=PARAMS,
        name="add_rows",
    )(member_far, returned)
    owned = lax.all_to_all(summed, far, 0, 0, tiled=True)
    grad_prefix_keys, grad_prefix_values = pl.pallas_call(
        sum_rows,
        in_specs=[vmem],
        out_specs=[vmem, vmem],
        out_shape=[jax.ShapeDtypeStruct((1, prefix_rows, HD), jnp.float32)] * 2,
        compiler_params=PARAMS,
        name="sum_rows",
    )(owned)

    grad_queries, grad_keys, grad_values = pl.pallas_call(
        functools.partial(own_grads, dims),
        grid_spec=pltpu.PrefetchScalarGridSpec(
            num_scalar_prefetch=1,
            grid=(kv_heads,),
            in_specs=[heads_q, heads_q, heads_k, heads_k, lanes, picked],
            out_specs=[heads_q, heads_k, heads_k],
            scratch_shapes=[packed, packed, bias],
        ),
        out_shape=[
            jax.ShapeDtypeStruct(queries.shape, jnp.bfloat16),
            jax.ShapeDtypeStruct(candidate_keys.shape, jnp.bfloat16),
            jax.ShapeDtypeStruct(candidate_values.shape, jnp.bfloat16),
        ],
        compiler_params=PARAMS,
        cost_estimate=cost(6 * big, 6 << 20),
        name="own_grads",
    )(meta, queries, grad_output, candidate_keys, candidate_values, total, pairs)
    return grad_queries, grad_keys, grad_values, grad_prefix_keys, grad_prefix_values


def solution(mesh, parts=(4, 2, 8)):
    seq = mesh.shape["seq"]
    inner = Mesh(mesh.devices.reshape(parts + (seq,)), ("zh", "zl", "y", "seq"))
    dp = ("zh", "zl", "y")
    both = dp + ("seq",)
    in_specs = (
        P(both, None, None),
        P(both, None, None),
        P(both, None, None),
        P(both, None, None),
        P(dp, None, "seq"),
        P(dp, None, "seq"),
        P(),
        P(),
        P(),
    )
    out_specs = (
        P(both, None, None),
        P(both, None, None),
        P(both, None, None),
        P(dp, None, "seq"),
        P(dp, None, "seq"),
    )
    return jax.shard_map(local, mesh=inner, in_specs=in_specs, out_specs=out_specs, check_vma=False)
```

time: 480 us -> 125 us (0.26)
  the two profiles are of different devices: /device:TPU:2 before, /device:TPU:8 now
where the time goes in v1:
time: 125 us
  waiting for transfers between devices  41.7 us (33%)
  starting transfers between devices  27.1 us (22%)
  Pallas kernels  21.5 us (17%)
  blocking collectives  15.7 us (13%)
  local copies, waits for them, and re-layouts  11.7 us (9%)
  between operations  4.72 us (4%)
  other arithmetic  2.21 us (2%)
    all_to_all x1, waiting for transfers between devices, local(): held = lax.all_to_all(everyone, far, 0, 0, tiled=True)  27.5 us
    all_to_all x1, starting transfers between devices, local(): held = lax.all_to_all(everyone, far, 0, 0, tiled=True)  16.2 us
    all_to_all x1, blocking collectives, local(): lax.all_to_all(terms.reshape(n_near, prefix_rows, 2 * HD), near, 0, 0, ti...  15.7 us
    all_to_all x1, waiting for transfers between devices, local(): owned = lax.all_to_all(summed, far, 0, 0, tiled=True)  14.2 us
    pallas_call x1, Pallas kernels, local(): pl.pallas_call(functools.partial(own_grads, dims), grid_spec=pltpu.Prefet...  9.91 us
    unnamed x28, local copies, waits for them, and re-layouts  7.52 us
    all_to_all x1, starting transfers between devices, local(): owned = lax.all_to_all(summed, far, 0, 0, tiled=True)  5.65 us
    all_to_all x1, starting transfers between devices, local(): pairs = lax.all_to_all(chosen, near, 0, 0, tiled=True)  5.3 us
  transfers between devices with their start and end apart: 3, of which 2 were waited for; matrix products, arithmetic and copies ran while one was open for 4% of the time, Pallas kernels for 11%

profile of v1, /device:TPU:8, one launch (start us, length us, event | category | flops | bytes accessed | tf_op | source)
XLA Modules:
  0.0 124.6 jit_solution(11821543686582239924)
XLA Ops:
  0.6 0.7 pad_maximum_fusion
  1.4 1.0 broadcast_in_dim.2
  2.4 16.2 %all-to-all-start = ((bf16[32,56,256]{2,1,0:T(8,128)(2,1)}), bf16[32,56,256]{2,1,0:T(8,128)(2,1)S(1)}, u32[]{:S(2)}, u32[]{:S(2)}) async-start(bf16[32,56,256]{2,1,0:T(8,128)(2,1)} %broadcast_in_dim.2), calls=%async_computation | async-start | bytes 1835008 | tf_op jit(solution)/shard_map/all_to_all | solution.py:232
  18.5 0.1 iota_add_fusion
  18.6 0.1 add.99
  18.7 0.0 copy-start.1
  18.7 0.7 gather_fusion
  19.4 27.5 %all-to-all-done.source = bf16[32,56,256]{2,1,0:T(8,128)(2,1)S(1)} async-done(((bf16[32,56,256]{2,1,0:T(8,128)(2,1)}), bf16[32,56,256]{2,1,0:T(8,128)(2,1)S(1)}, u32[]{:S(2)}, u32[]{:S(2)}) %all-to-all-start) | async-done | bytes 917536 | tf_op jit(solution)/shard_map/all_to_all | solution.py:232
  47.0 1.3 %pick_rows.1 = bf16[16,56,256]{2,1,0:T(8,128)(2,1)S(1)} custom-call(s32[16]{0:T(128)S(1)} %fusion.index, bf16[32,56,256]{2,1,0:T(8,128)(2,1)S(1)} %all-to-all-done.source), custom_call_target="tpu_custom_call" | custom-call | tf_op jit(solution)/shard_map/pick_rows/pallas_call | solution.py:247
  48.3 0.0 copy-start.5
  48.3 0.8 copy-done.5
  49.1 5.3 %all-to-all-start.1 = ((bf16[16,56,256]{2,1,0:T(8,128)(2,1)}), bf16[16,56,256]{2,1,0:T(8,128)(2,1)S(1)}, u32[]{:S(2)}, u32[]{:S(2)}) async-start(bf16[16,56,256]{2,1,0:T(8,128)(2,1)} %copy-done.5), calls=%async_computation.1 | async-start | bytes 917504 | tf_op jit(solution)/shard_map/all_to_all | solution.py:256
  54.4 0.6 dynamic_slice.10
  58.9 1.3 %dynamic_slice.9 = s32[1]{0:T(128)} dynamic-slice(s32[512]{0:T(512)} %param.16, s32[]{:T(128)S(6)} %select_n.42), dynamic_slice_sizes={1} | dynamic-slice | bytes 12 | tf_op jit(solution)/shard_map/dynamic_slice | solution.py:214
  60.2 0.6 dynamic_slice.11
  60.8 1.4 %pad_add_fusion.meta = s32[3]{0:T(128)S(1)} fusion(s32[1]{0:T(128)} %bitcast.1, s32[1]{0:T(128)} %dynamic_slice.11, s32[1]{0:T(128)} %dynamic_slice.9), kind=kLoop, calls=%fused_computation.16 | loop fusion | flops 6 | bytes 24 | tf_op jit(solution)/shard_map/stack | solution.py:214
  62.1 1.0 copy-done.6
  63.1 1.0 copy-done.8
  64.1 3.8 %own_stats.1.stats = f32[8,8,640]{2,1,0:T(8,128)S(1)} custom-call(s32[3]{0:T(128)S(1)} %pad_add_fusion.meta, bf16[1,152,4096]{2,1,0:T(8,128)(2,1)S(1)} %copy-done, bf16[1,152,4096]{2,1,0:T(8,128)(2,1)S(1)} %copy-done.1, bf16[1,152,1024]{2,1,0:T(8,128)(2,1)S(1)} %copy-done.6, bf16[1,152,1024]{2,1,0:T(8,128)(2,1)S(1)} %copy-done.8), custom_call_target="tpu_custom_call" | custom-call | flops 398458880 | bytes 3145728 | tf_op jit(solution)/shard_map/own_stats/pallas_call | solution.py:233
  67.9 0.0 copy-start.3
  67.9 4.8 %prefix_terms.1 = (f32[8,8,640]{2,1,0:T(8,128)S(1)}, bf16[2,8,56,256]{3,2,1,0:T(8,128)(2,1)S(1)}) custom-call(s32[3]{0:T(128)S(1)} %pad_add_fusion.meta, bf16[1,152,4096]{2,1,0:T(8,128)(2,1)S(1)} %copy-done, bf16[1,152,4096]{2,1,0:T(8,128)(2,1)S(1)} %copy-done.1, f32[8,8,640]{2,1,0:T(8,128)S(1)} %own_stats.1.stats, bf16[16,56,256]{2,1,0:T(8,128)(2,1)S(1)} %all-to-all-done.1.pair), custom_call_target="tpu_custom_call" | custom-call | flops 398458880 | bytes 3145728 | tf_op jit(solution)/shard_map/prefix_terms/pallas_call | solution.py:258
  72.8 15.7 %all_to_all.20.source = bf16[16,56,256]{2,1,0:T(8,128)(2,1)S(1)} all-to-all(bf16[16,56,256]{2,1,0:T(8,128)(2,1)S(1)} %bitcast.7), channel_id=1, replica_groups=mesh['zh'=4,'zl'=2,'y'=8,'seq'=8] {'zl','seq'}, dimensions={0} | all-to-all | bytes 917504 | tf_op jit(solution)/shard_map/all_to_all | solution.py:279
  88.4 0.9 add_rows.1
  89.3 0.9 copy-done.2
  90.2 5.6 %all-to-all-start.3 = ((bf16[32,56,256]{2,1,0:T(8,128)(2,1)}), bf16[32,56,256]{2,1,0:T(8,128)(2,1)S(1)}, u32[]{:S(2)}, u32[]{:S(2)}) async-start(bf16[32,56,256]{2,1,0:T(8,128)(2,1)} %copy-done.2), calls=%async_computation.3 | async-start | bytes 1835008 | tf_op jit(solution)/shard_map/all_to_all | solution.py:291
  95.9 1.0 copy-done.4
  96.9 1.0 copy-done.7
  97.9 1.0 copy-done.9
  98.9 0.9 copy-done.11
  99.8 9.9 %own_grads.1 = (bf16[1,152,4096]{2,1,0:T(8,128)(2,1)}, bf16[1,152,1024]{2,1,0:T(8,128)(2,1)}, bf16[1,152,1024]{2,1,0:T(8,128)(2,1)}) custom-call(s32[3]{0:T(128)S(1)} %pad_add_fusion.meta, bf16[1,152,4096]{2,1,0:T(8,128)(2,1)S(1)} %copy-done, bf16[1,152,4096]{2,1,0:T(8,128)(2,1)S(1)} %copy-done.1, bf16[1,152,1024]{2,1,0:T(8,128)(2,1)S(1)} %copy-done.7, ...), custom_call_target="tpu_custom_call" | custom-call | flops 1195376640 | bytes 6291456 | tf_op jit(solution)/shard_map/own_grads/pallas_call | solution.py:301
  109.7 14.2 %all-to-all-done.3.source = bf16[32,56,256]{2,1,0:T(8,128)(2,1)S(1)} async-done(((bf16[32,56,256]{2,1,0:T(8,128)(2,1)}), bf16[32,56,256]{2,1,0:T(8,128)(2,1)S(1)}, u32[]{:S(2)}, u32[]{:S(2)}) %all-to-all-start.3) | async-done | bytes 917536 | tf_op jit(solution)/shard_map/all_to_all | solution.py:291
  123.9 0.7 sum_rows.1
  (22 shorter events, 0.1 us)
Async XLA Ops:
  1.4 17.4 %copy-start.12 = (s32[512]{0:T(512)S(1)}, s32[512]{0:T(512)}, u32[]{:S(2)}) copy-start(s32[512]{0:T(512)} %param.15) | copy-start | bytes 6148
  2.4 44.6 %all-to-all-start = ((bf16[32,56,256]{2,1,0:T(8,128)(2,1)}), bf16[32,56,256]{2,1,0:T(8,128)(2,1)S(1)}, u32[]{:S(2)}, u32[]{:S(2)}) async-start(bf16[32,56,256]{2,1,0:T(8,128)(2,1)} %broadcast_in_dim.2), calls=%async_computation | async-start | bytes 1835008 | tf_op jit(solution)/shard_map/all_to_all | solution.py:232
  18.7 43.4 %copy-start.1 = (bf16[1,152,4096]{2,1,0:T(8,128)(2,1)S(1)}, bf16[1,152,4096]{2,1,0:T(8,128)(2,1)}, u32[]{:S(2)}) copy-start(bf16[1,152,4096]{2,1,0:T(8,128)(2,1)} %g.5) | copy-start | bytes 3735556
  19.4 40.8 %copy-start.13 = (s32[64]{0:T(128)S(1)}, s32[64]{0:T(128)}, u32[]{:S(2)}) copy-start(s32[64]{0:T(128)} %param.17) | copy-start | bytes 772
  19.4 42.7 %copy-start = (bf16[1,152,4096]{2,1,0:T(8,128)(2,1)S(1)}, bf16[1,152,4096]{2,1,0:T(8,128)(2,1)}, u32[]{:S(2)}) copy-start(bf16[1,152,4096]{2,1,0:T(8,128)(2,1)} %q.5) | copy-start | bytes 3735556
  48.3 0.8 copy-start.5
  49.1 18.8 %all-to-all-start.1 = ((bf16[16,56,256]{2,1,0:T(8,128)(2,1)}), bf16[16,56,256]{2,1,0:T(8,128)(2,1)S(1)}, u32[]{:S(2)}, u32[]{:S(2)}) async-start(bf16[16,56,256]{2,1,0:T(8,128)(2,1)} %copy-done.5), calls=%async_computation.1 | async-start | bytes 917504 | tf_op jit(solution)/shard_map/all_to_all | solution.py:256
  62.1 1.0 copy-start.6
  63.1 1.0 copy-start.8
  67.9 4.8 %copy-start.3 = (bf16[16,56,256]{2,1,0:T(8,128)(2,1)}, bf16[16,56,256]{2,1,0:T(8,128)(2,1)S(1)}, u32[]{:S(2)}) copy-start(bf16[16,56,256]{2,1,0:T(8,128)(2,1)S(1)} %all-to-all-done.1.pair) | copy-start | bytes 1376260
  72.8 17.5 %copy-start.10 = (f32[8,8,640]{2,1,0:T(8,128)}, f32[8,8,640]{2,1,0:T(8,128)S(1)}, u32[]{:S(2)}) copy-start(f32[8,8,640]{2,1,0:T(8,128)S(1)} %get-tuple-element.12.total) | copy-start | bytes 491524
  89.3 0.9 copy-start.2
  90.2 33.6 %all-to-all-start.3 = ((bf16[32,56,256]{2,1,0:T(8,128)(2,1)}), bf16[32,56,256]{2,1,0:T(8,128)(2,1)S(1)}, u32[]{:S(2)}, u32[]{:S(2)}) async-start(bf16[32,56,256]{2,1,0:T(8,128)(2,1)} %copy-done.2), calls=%async_computation.3 | async-start | bytes 1835008 | tf_op jit(solution)/shard_map/all_to_all | solution.py:291
  95.9 1.0 copy-start.4
  96.9 1.0 copy-start.7
  97.9 1.0 copy-start.9
  98.8 0.9 copy-start.11

commit v2 on v1

v2 whole, which is shorter than its diff:
```python
import functools
import math

import jax
import jax.numpy as jnp
from jax import lax
from jax.experimental import pallas as pl
from jax.experimental.pallas import tpu as pltpu
from jax.sharding import Mesh, PartitionSpec as P

HD = 128
PAD = 16
NEG = -1e30
VMEM = 60 * 1024 * 1024


def stack_heads(ref, out, part, rows, group, stride):
    for h in range(group):
        lanes = slice((part * group + h) * HD, (part * group + h + 1) * HD)
        out[part, pl.ds(h * stride, rows), :] = ref[0, :, lanes]


def dot_nt(a, b):
    return lax.dot_general(a, b, (((1,), (1,)), ((), ())), preferred_element_type=jnp.float32)


def dot_nn(a, b):
    return lax.dot_general(a, b, (((1,), (0,)), ((), ())), preferred_element_type=jnp.float32)


def dot_tn(a, b):
    return lax.dot_general(a, b, (((0,), (0,)), ((), ())), preferred_element_type=jnp.float32)


def own_bias(bias, length, rows, group, stride):
    inside = lax.broadcasted_iota(jnp.int32, (rows, stride), 0)
    row = lax.broadcasted_iota(jnp.int32, (rows, stride), 1)
    tile = jnp.where(jnp.logical_and(inside <= row, inside < length), 0.0, NEG)
    bias[...] = jnp.concatenate([tile] * group, axis=1)


def prologue(q4, g4):
    q4[...] = jnp.zeros_like(q4)
    g4[...] = jnp.zeros_like(g4)


def own_stats(dims, skips, where, index, lengths, prefixes, q, g, k, v, *refs):
    meta, members, stats, q4, g4, bias = refs
    rows, group, stride, factor, _ = dims

    @pl.when(pl.program_id(0) == 0)
    def _():
        length = lengths[where[1]]
        meta[0] = length
        meta[1] = prefixes[index[where[1]]]
        for i, skip in enumerate(skips):
            members[i] = index[where[0] + skip]
        prologue(q4, g4)
        own_bias(bias, length, rows, group, stride)

    for part in range(q4.shape[0]):
        stack_heads(q, q4, part, rows, group, stride)
        stack_heads(g, g4, part, rows, group, stride)
        lanes = slice(part * HD, (part + 1) * HD)
        scores = dot_nt(k[0, :, lanes], q4[part]) * factor + bias[...]
        highest = jnp.max(scores, axis=0, keepdims=True)
        expon = jnp.exp2(scores - highest)
        grad_probs = dot_nt(v[0, :, lanes], g4[part])
        stats[part, 0:1, :] = highest
        stats[part, 1:2, :] = jnp.sum(expon, axis=0, keepdims=True)
        stats[part, 2:3, :] = jnp.sum(expon * grad_probs, axis=0, keepdims=True)


def live_lanes(length, group, stride):
    row = lax.broadcasted_iota(jnp.int32, (1, stride), 1)
    live = jnp.where(row < length, 1.0, 0.0)
    return jnp.concatenate([live] * group, axis=1)


def prefix_bias(prefix_length, prefix_rows, width):
    column = lax.broadcasted_iota(jnp.int32, (prefix_rows, width), 0)
    return jnp.where(column < prefix_length, 0.0, NEG)


def prefix_terms(dims, meta, q, g, stats, pair, total, terms, q4, g4):
    rows, group, stride, factor, scale = dims
    half = pair.shape[0] // 2
    prefix_rows = half * pair.shape[2]

    @pl.when(pl.program_id(0) == 0)
    def _():
        prologue(q4, g4)

    mask = prefix_bias(meta[1], prefix_rows, group * stride)
    live = live_lanes(meta[0], group, stride)
    for part in range(q4.shape[0]):
        stack_heads(q, q4, part, rows, group, stride)
        stack_heads(g, g4, part, rows, group, stride)
        keys = pair[0:half, part].reshape(prefix_rows, HD)
        values = pair[half:, part].reshape(prefix_rows, HD)
        scores = dot_nt(keys, q4[part]) * factor + mask
        own_high = stats[part, 0:1, :]
        highest = jnp.maximum(own_high, jnp.max(scores, axis=0, keepdims=True))
        expon = jnp.exp2(scores - highest)
        fade = jnp.exp2(own_high - highest)
        weight = fade * stats[part, 1:2, :] + jnp.sum(expon, axis=0, keepdims=True)
        inverse = live / weight
        grad_probs = dot_nt(values, g4[part])
        delta = fade * stats[part, 2:3, :] + jnp.sum(expon * grad_probs, axis=0, keepdims=True)
        delta = delta * inverse
        probs = expon * inverse
        grad_scores = (probs * (grad_probs - delta) * scale).astype(jnp.bfloat16)
        total[part, 0:1, :] = highest
        total[part, 1:2, :] = inverse
        total[part, 2:3, :] = delta
        key_terms = dot_nn(grad_scores, q4[part])
        value_terms = dot_nn(probs.astype(jnp.bfloat16), g4[part])
        terms[0:half, part] = key_terms.astype(jnp.bfloat16).reshape((half,) + terms.shape[2:])
        terms[half:, part] = value_terms.astype(jnp.bfloat16).reshape((half,) + terms.shape[2:])


def own_grads(dims, meta, q, g, k, v, total, pair, dq, dk, dv, q4, g4, bias):
    rows, group, stride, factor, scale = dims
    half = pair.shape[0] // 2
    prefix_rows = half * pair.shape[2]

    @pl.when(pl.program_id(0) == 0)
    def _():
        prologue(q4, g4)
        own_bias(bias, meta[0], rows, group, stride)

    prefix_mask = prefix_bias(meta[1], prefix_rows, group * stride)
    for part in range(q4.shape[0]):
        stack_heads(q, q4, part, rows, group, stride)
        stack_heads(g, g4, part, rows, group, stride)
        highest = total[part, 0:1, :]
        inverse = total[part, 1:2, :]
        delta = total[part, 2:3, :]

        def one(keys, values, mask):
            scores = dot_nt(keys, q4[part]) * factor + mask
            probs = jnp.exp2(scores - highest) * inverse
            grad_probs = dot_nt(values, g4[part])
            return probs, (probs * (grad_probs - delta) * scale).astype(jnp.bfloat16)

        keys = pair[0:half, part].reshape(prefix_rows, HD)
        values = pair[half:, part].reshape(prefix_rows, HD)
        here = slice(part * HD, (part + 1) * HD)
        _, prefix_scores = one(keys, values, prefix_mask)
        probs, grad_scores = one(k[0, :, here], v[0, :, here], bias[...])
        dv[0, :, here] = dot_nn(probs.astype(jnp.bfloat16), g4[part]).astype(jnp.bfloat16)
        dk[0, :, here] = dot_nn(grad_scores, q4[part]).astype(jnp.bfloat16)
        for h in range(group):
            lanes = slice(h * stride, (h + 1) * stride)
            rows_q = dot_tn(grad_scores[:, lanes], k[0, :, here])
            rows_q = rows_q + dot_tn(prefix_scores[:, lanes], keys)
            at = part * group + h
            dq[0, :, at * HD : (at + 1) * HD] = rows_q[:rows].astype(jnp.bfloat16)


def spread(places, keys, values, out, whole):
    prefix_rows = keys.shape[1]
    piece = out.shape[1]
    whole[...] = jnp.zeros_like(whole)
    whole[0:prefix_rows, :] = keys[0]
    middle = whole.shape[0] // 2
    whole[middle : middle + prefix_rows, :] = values[0]
    for i, place in enumerate(places):
        out[i] = whole[place * piece : (place + 1) * piece, :]


def pick_rows(members, source, out):
    for i in range(out.shape[0]):
        out[i] = source[members[i]]


def add_rows(members, source, out, acc):
    acc[...] = jnp.zeros_like(acc)
    for i in range(source.shape[0]):
        at = members[i]
        acc[at] = acc[at] + source[i].astype(jnp.float32)
    out[...] = acc[...].astype(jnp.bfloat16)


def sum_rows(places, source, keys, values):
    piece = source.shape[1]
    count = max(places) + 1
    totals = [None] * count
    for i, place in enumerate(places):
        row = source[i].astype(jnp.float32)
        totals[place] = row if totals[place] is None else totals[place] + row
    for place, total in enumerate(totals):
        out = keys if place < count // 2 else values
        at = (place % (count // 2)) * piece
        size = max(0, min(piece, out.shape[1] - at))
        if size:
            out[0, at : at + size, :] = total[:size]


PARAMS = pltpu.CompilerParams(vmem_limit_bytes=VMEM)


def cost(flops, nbytes):
    return pl.CostEstimate(flops=flops, bytes_accessed=nbytes, transcendentals=flops // 256)


def local(
    queries,
    candidate_keys,
    candidate_values,
    grad_output,
    prefix_keys,
    prefix_values,
    query_index,
    candidate_length,
    prefix_length,
):
    far, near, seq = ("zh", "zl", "yh", "yl"), ("zl", "yl", "seq"), "seq"
    rows, width_q = queries.shape[1:]
    kv_heads = candidate_keys.shape[2] // HD
    group = width_q // (kv_heads * HD)
    prefix_rows = prefix_keys.shape[1]
    stride = -(-rows // PAD) * PAD
    width = group * stride
    scale = 1.0 / math.sqrt(HD)
    dims = (rows, group, stride, scale * math.log2(math.e), scale)
    sizes = tuple(lax.axis_size(a) for a in far)
    size_zh, size_zl, size_yh, size_yl = sizes
    size_s = lax.axis_size(seq)
    pieces = size_zl * size_yl
    n_far, n_near = size_zh * size_zl * size_yh * size_yl, pieces * size_s
    half = pieces // 2
    piece = -(-prefix_rows // (half * PAD)) * PAD
    places = tuple(
        ((i // (size_yl * size_yh)) % size_zl) * size_yl + i % size_yl for i in range(n_far)
    )
    skips = tuple(
        (zl * size_yh * size_yl + yl) * size_s + s
        for zl in range(size_zl)
        for yl in range(size_yl)
        for s in range(size_s)
    )
    zh, zl, yh, yl, s = (lax.axis_index(a) for a in far + (seq,))
    first = (zh * size_zl * size_yh + yh) * size_yl * size_s
    mine = first + (zl * size_yh * size_yl + yl) * size_s + s
    where = jnp.stack([first, mine]).astype(jnp.int32)

    smem = pl.BlockSpec(memory_space=pltpu.SMEM)
    vmem = pl.BlockSpec(memory_space=pltpu.VMEM)
    per = 2 if kv_heads % 2 == 0 else 1
    steps = kv_heads // per
    per = 2 if kv_heads % 2 == 0 else 1
    steps = kv_heads // per
    heads_q = pl.BlockSpec((1, rows, per * group * HD), lambda i: (0, 0, i))
    heads_k = pl.BlockSpec((1, rows, per * HD), lambda i: (0, 0, i))
    lanes = pl.BlockSpec((per, 8, width), lambda i: (i, 0, 0))
    parted = pl.BlockSpec((pieces, per, piece, HD), lambda i: (0, i, 0, 0))
    packed = pltpu.VMEM((per, width, HD), jnp.bfloat16)
    bias = pltpu.VMEM((rows, width), jnp.float32)
    lane_shape = jax.ShapeDtypeStruct((kv_heads, 8, width), jnp.float32)
    far_shape = (n_far, piece, HD)
    near_shape = (n_near, piece, HD)
    part_shape = (pieces, kv_heads, piece, HD)
    big = kv_heads * width * rows * HD * 2

    everyone = pl.pallas_call(
        functools.partial(spread, places),
        in_specs=[vmem, vmem],
        out_specs=vmem,
        out_shape=jax.ShapeDtypeStruct(far_shape, jnp.bfloat16),
        scratch_shapes=[pltpu.VMEM((pieces * piece, HD), jnp.bfloat16)],
        compiler_params=PARAMS,
        name="spread",
    )(prefix_keys, prefix_values)
    held = lax.all_to_all(everyone, far, 0, 0, tiled=True)
    meta, members, stats = pl.pallas_call(
        functools.partial(own_stats, dims, skips),
        grid=(steps,),
        in_specs=[smem, smem, smem, smem, heads_q, heads_q, heads_k, heads_k],
        out_specs=[smem, smem, lanes],
        scratch_shapes=[packed, packed, bias],
        out_shape=[
            jax.ShapeDtypeStruct((2,), jnp.int32),
            jax.ShapeDtypeStruct((n_near,), jnp.int32),
            lane_shape,
        ],
        compiler_params=PARAMS,
        cost_estimate=cost(2 * big, 3 << 20),
        name="own_stats",
    )(
        where,
        query_index,
        candidate_length,
        prefix_length,
        queries,
        grad_output,
        candidate_keys,
        candidate_values,
    )
    chosen = pl.pallas_call(
        pick_rows,
        in_specs=[smem, vmem],
        out_specs=vmem,
        out_shape=jax.ShapeDtypeStruct(near_shape, jnp.bfloat16),
        compiler_params=PARAMS,
        name="pick_rows",
    )(members, held)
    pairs = lax.all_to_all(chosen, near, 0, 0, tiled=True).reshape(part_shape)

    total, terms = pl.pallas_call(
        functools.partial(prefix_terms, dims),
        grid=(steps,),
        in_specs=[smem, heads_q, heads_q, lanes, parted],
        out_specs=[lanes, parted],
        scratch_shapes=[packed, packed],
        out_shape=[lane_shape, jax.ShapeDtypeStruct(part_shape, jnp.bfloat16)],
        compiler_params=PARAMS,
        cost_estimate=cost(2 * big, 3 << 20),
        name="prefix_terms",
    )(meta, queries, grad_output, stats, pairs)

    returned = lax.all_to_all(terms.reshape(near_shape), near, 0, 0, tiled=True)
    summed = pl.pallas_call(
        add_rows,
        in_specs=[smem, vmem],
        out_specs=vmem,
        out_shape=jax.ShapeDtypeStruct(far_shape, jnp.bfloat16),
        scratch_shapes=[pltpu.VMEM(far_shape, jnp.float32)],
        compiler_params=PARAMS,
        name="add_rows",
    )(members, returned)
    owned = lax.all_to_all(summed, far, 0, 0, tiled=True)
    grad_prefix_keys, grad_prefix_values = pl.pallas_call(
        functools.partial(sum_rows, places),
        in_specs=[vmem],
        out_specs=[vmem, vmem],
        out_shape=[jax.ShapeDtypeStruct((1, prefix_rows, HD), jnp.float32)] * 2,
        compiler_params=PARAMS,
        name="sum_rows",
    )(owned)

    grad_queries, grad_keys, grad_values = pl.pallas_call(
        functools.partial(own_grads, dims),
        grid=(steps,),
        in_specs=[smem, heads_q, heads_q, heads_k, heads_k, lanes, parted],
        out_specs=[heads_q, heads_k, heads_k],
        scratch_shapes=[packed, packed, bias],
        out_shape=[
            jax.ShapeDtypeStruct(queries.shape, jnp.bfloat16),
            jax.ShapeDtypeStruct(candidate_keys.shape, jnp.bfloat16),
            jax.ShapeDtypeStruct(candidate_values.shape, jnp.bfloat16),
        ],
        compiler_params=PARAMS,
        cost_estimate=cost(6 * big, 6 << 20),
        name="own_grads",
    )(meta, queries, grad_output, candidate_keys, candidate_values, total, pairs)
    return grad_queries, grad_keys, grad_values, grad_prefix_keys, grad_prefix_values


def solution(mesh, parts=(4, 2, 2, 4)):
    seq = mesh.shape["seq"]
    inner = Mesh(mesh.devices.reshape(parts + (seq,)), ("zh", "zl", "yh", "yl", "seq"))
    dp = ("zh", "zl", "yh", "yl")
    both = dp + ("seq",)
    in_specs = (
        P(both, None, None),
        P(both, None, None),
        P(both, None, None),
        P(both, None, None),
        P(dp, None, "seq"),
        P(dp, None, "seq"),
        P(),
        P(),
        P(),
    )
    out_specs = (
        P(both, None, None),
        P(both, None, None),
        P(both, None, None),
        P(dp, None, "seq"),
        P(dp, None, "seq"),
    )
    return jax.shard_map(local, mesh=inner, in_specs=in_specs, out_specs=out_specs, check_vma=False)
```

time: 125 us -> 102 us (0.82)
  waiting for transfers between devices: 41.7 us -> 14.8 us
  blocking collectives: 15.7 us -> 34.9 us
  local copies, waits for them, and re-layouts: 11.7 us -> 1.4 us
  Pallas kernels: 21.5 us -> 25.8 us
  between operations: 4.72 us -> 0.67 us
  starting transfers between devices: 27.1 us -> 23.5 us
  other arithmetic: 2.21 us -> 0.59 us
    all_to_all x1 -> x2, blocking collectives: 15.7 us -> 34.9 us  [the longest x1 18 us: local(): pairs = lax.all_to_all(chosen, near, 0, 0, tiled=True).reshape(part_shape)]
    all_to_all x1, waiting for transfers between devices: 27.5 us -> 9.04 us  [local(): held = lax.all_to_all(everyone, far, 0, 0, tiled=True)]
    all_to_all x1, waiting for transfers between devices: 14.2 us -> 5.73 us  [local(): owned = lax.all_to_all(summed, far, 0, 0, tiled=True)]
    unnamed x28 -> x4, local copies, waits for them, and re-layouts: 7.52 us -> 1.4 us
    all_to_all x1 -> x0, starting transfers between devices: 5.3 us -> none  [local(): pairs = lax.all_to_all(chosen, near, 0, 0, tiled=True)]
    pallas_call x5 -> x6, Pallas kernels: 20.6 us -> 23.9 us  [the longest x1 8.86 us: local(): pl.pallas_call(functools.partial(own_grads, dims), grid=(steps,), in_spec...]
    dynamic_slice x3 -> x0, local copies, waits for them, and re-layouts: 2.44 us -> none  [the longest x1 1.27 us: local(): candidate_length[mine]]
    all_to_all x1, starting transfers between devices: 5.65 us -> 6.95 us  [local(): owned = lax.all_to_all(summed, far, 0, 0, tiled=True)]
  transfers between devices with their start and end apart: 3 -> 2, of which waited for: 2 -> 2; matrix products, arithmetic and copies ran while one was open for 4% -> 1% of each run, Pallas kernels for 11% -> 13%
where the time goes in v2:
time: 102 us
  blocking collectives  34.9 us (34%)
  Pallas kernels  25.8 us (25%)
  starting transfers between devices  23.5 us (23%)
  waiting for transfers between devices  14.8 us (15%)
  local copies, waits for them, and re-layouts  1.4 us (1%)
    all_to_all x1, blocking collectives, local(): pairs = lax.all_to_all(chosen, near, 0, 0, tiled=True).reshape(part_shape)  18 us
    all_to_all x1, blocking collectives, local(): returned = lax.all_to_all(terms.reshape(near_shape), near, 0, 0, tiled=True)  16.9 us
    all_to_all x1, starting transfers between devices, local(): held = lax.all_to_all(everyone, far, 0, 0, tiled=True)  16.6 us
    all_to_all x1, waiting for transfers between devices, local(): held = lax.all_to_all(everyone, far, 0, 0, tiled=True)  9.04 us
    pallas_call x1, Pallas kernels, local(): pl.pallas_call(functools.partial(own_grads, dims), grid=(steps,), in_spec...  8.86 us
    all_to_all x1, starting transfers between devices, local(): owned = lax.all_to_all(summed, far, 0, 0, tiled=True)  6.95 us
    all_to_all x1, waiting for transfers between devices, local(): owned = lax.all_to_all(summed, far, 0, 0, tiled=True)  5.73 us
    pallas_call x1, Pallas kernels, local(): pl.pallas_call(functools.partial(prefix_terms, dims), grid=(steps,), in_s...  5.55 us
  transfers between devices with their start and end apart: 2, of which 2 were waited for; matrix products, arithmetic and copies ran while one was open for 1% of the time, Pallas kernels for 13%

profile of v2, /device:TPU:8, one launch (start us, length us, event | category | flops | bytes accessed | tf_op | source)
XLA Modules:
  0.0 101.6 jit_solution(13461647649212197517)
XLA Ops:
  0.6 1.5 %spread.1 = bf16[64,16,128]{2,1,0:T(8,128)(2,1)} custom-call(bf16[1,56,128]{2,1,0:T(8,128)(2,1)} %keys.1, bf16[1,56,128]{2,1,0:T(8,128)(2,1)} %values.1), custom_call_target="tpu_custom_call" | custom-call | tf_op jit(solution)/shard_map/spread/pallas_call | solution.py:266
  2.1 16.6 %all-to-all-start = ((bf16[64,16,128]{2,1,0:T(8,128)(2,1)}), bf16[64,16,128]{2,1,0:T(8,128)(2,1)S(1)}, u32[]{:S(2)}, u32[]{:S(2)}) async-start(bf16[64,16,128]{2,1,0:T(8,128)(2,1)} %spread.1), calls=%async_computation | async-start | bytes 524288 | tf_op jit(solution)/shard_map/all_to_all | solution.py:275
  18.7 0.6 pad_add_fusion.where
  19.3 4.7 %own_stats.1 = (s32[2]{0:T(128)}, s32[64]{0:T(128)}, f32[8,8,640]{2,1,0:T(8,128)}) custom-call(s32[2]{0:T(128)} %pad_add_fusion.where, s32[512]{0:T(512)} %index.1, s32[512]{0:T(512)} %lengths.1, s32[64]{0:T(128)} %prefixes.1, bf16[1,152,4096]{2,1,0:T(8,128)(2,1)} %q.5, bf16[1,152,4096]{2,1,0:T(8,128)(2,1)} %g.5, bf16[1,152,1024]{2,1,0:T(8,128)(2,1)} %k.3, ...), custom_call_target="tpu_custom_call" | custom-call | flops 398458880 | bytes 3145728 | tf_op jit(solution)/shard_map/own_stats/pallas_call | solution.py:276
  24.0 9.0 %all-to-all-done.source = bf16[64,16,128]{2,1,0:T(8,128)(2,1)S(1)} async-done(((bf16[64,16,128]{2,1,0:T(8,128)(2,1)}), bf16[64,16,128]{2,1,0:T(8,128)(2,1)S(1)}, u32[]{:S(2)}, u32[]{:S(2)}) %all-to-all-start) | async-done | bytes 262176 | tf_op jit(solution)/shard_map/all_to_all | solution.py:275
  33.0 0.0 copy-start
  33.0 0.7 copy-done
  33.7 1.7 %pick_rows.1 = bf16[64,16,128]{2,1,0:T(8,128)(2,1)} custom-call(s32[64]{0:T(128)} %get-tuple-element.17.members, bf16[64,16,128]{2,1,0:T(8,128)(2,1)} %copy-done), custom_call_target="tpu_custom_call" | custom-call | tf_op jit(solution)/shard_map/pick_rows/pallas_call | solution.py:300
  35.4 18.0 %all_to_all.20 = bf16[64,16,128]{2,1,0:T(8,128)(2,1)} all-to-all(bf16[64,16,128]{2,1,0:T(8,128)(2,1)} %pick_rows.1), channel_id=1, replica_groups=mesh['zh'=4,'zl'=2,'yh'=2,'yl'=4,'seq'=8] {'zl','yl','seq'}, dimensions={0} | all-to-all | bytes 524288 | tf_op jit(solution)/shard_map/all_to_all | solution.py:308
  53.4 5.5 %prefix_terms.1 = (f32[8,8,640]{2,1,0:T(8,128)}, bf16[8,8,16,128]{3,2,1,0:T(8,128)(2,1)}) custom-call(s32[2]{0:T(128)} %get-tuple-element.15.meta, bf16[1,152,4096]{2,1,0:T(8,128)(2,1)} %q.5, bf16[1,152,4096]{2,1,0:T(8,128)(2,1)} %g.5, f32[8,8,640]{2,1,0:T(8,128)} %get-tuple-element.16.stats, bf16[8,8,16,128]{3,2,1,0:T(8,128)(2,1)} %bitcast.4), custom_call_target="tpu_custom_call" | custom-call | flops 398458880 | bytes 3145728 | tf_op jit(solution)/shard_map/prefix_terms/pallas_call | solution.py:310
  59.0 16.9 %all_to_all.21.source = bf16[64,16,128]{2,1,0:T(8,128)(2,1)} all-to-all(bf16[64,16,128]{2,1,0:T(8,128)(2,1)} %bitcast.6), channel_id=1, replica_groups=mesh['zh'=4,'zl'=2,'yh'=2,'yl'=4,'seq'=8] {'zl','yl','seq'}, dimensions={0} | all-to-all | bytes 524288 | tf_op jit(solution)/shard_map/all_to_all | solution.py:322
  75.9 1.9 %add_rows.1 = bf16[64,16,128]{2,1,0:T(8,128)(2,1)} custom-call(s32[64]{0:T(128)} %get-tuple-element.17.members, bf16[64,16,128]{2,1,0:T(8,128)(2,1)} %all_to_all.21.source), custom_call_target="tpu_custom_call" | custom-call | tf_op jit(solution)/shard_map/add_rows/pallas_call | solution.py:323
  77.8 6.9 %all-to-all-start.3 = ((bf16[64,16,128]{2,1,0:T(8,128)(2,1)}), bf16[64,16,128]{2,1,0:T(8,128)(2,1)S(1)}, u32[]{:S(2)}, u32[]{:S(2)}) async-start(bf16[64,16,128]{2,1,0:T(8,128)(2,1)} %add_rows.1), calls=%async_computation.3 | async-start | bytes 524288 | tf_op jit(solution)/shard_map/all_to_all | solution.py:332
  84.7 8.9 %own_grads.1 = (bf16[1,152,4096]{2,1,0:T(8,128)(2,1)}, bf16[1,152,1024]{2,1,0:T(8,128)(2,1)}, bf16[1,152,1024]{2,1,0:T(8,128)(2,1)}) custom-call(s32[2]{0:T(128)} %get-tuple-element.15.meta, bf16[1,152,4096]{2,1,0:T(8,128)(2,1)} %q.5, bf16[1,152,4096]{2,1,0:T(8,128)(2,1)} %g.5, bf16[1,152,1024]{2,1,0:T(8,128)(2,1)} %k.3, bf16[1,152,1024]{2,1,0:T(8,128)(2,1)} %v.3, ...), custom_call_target="tpu_custom_call" | custom-call | flops 1195376640 | bytes 6291456 | tf_op jit(solution)/shard_map/own_grads/pallas_call | solution.py:342
  93.6 5.7 %all-to-all-done.3.source = bf16[64,16,128]{2,1,0:T(8,128)(2,1)S(1)} async-done(((bf16[64,16,128]{2,1,0:T(8,128)(2,1)}), bf16[64,16,128]{2,1,0:T(8,128)(2,1)S(1)}, u32[]{:S(2)}, u32[]{:S(2)}) %all-to-all-start.3) | async-done | bytes 262176 | tf_op jit(solution)/shard_map/all_to_all | solution.py:332
  99.3 0.0 copy-start.1
  99.3 0.7 copy-done.1
  100.0 1.6 %sum_rows.1 = (f32[1,56,128]{2,1,0:T(8,128)}, f32[1,56,128]{2,1,0:T(8,128)}) custom-call(bf16[64,16,128]{2,1,0:T(8,128)(2,1)} %copy-done.1), custom_call_target="tpu_custom_call" | custom-call | tf_op jit(solution)/shard_map/sum_rows/pallas_call | solution.py:333
Async XLA Ops:
  2.1 30.9 %all-to-all-start = ((bf16[64,16,128]{2,1,0:T(8,128)(2,1)}), bf16[64,16,128]{2,1,0:T(8,128)(2,1)S(1)}, u32[]{:S(2)}, u32[]{:S(2)}) async-start(bf16[64,16,128]{2,1,0:T(8,128)(2,1)} %spread.1), calls=%async_computation | async-start | bytes 524288 | tf_op jit(solution)/shard_map/all_to_all | solution.py:275
  33.0 0.7 copy-start
  77.8 21.6 %all-to-all-start.3 = ((bf16[64,16,128]{2,1,0:T(8,128)(2,1)}), bf16[64,16,128]{2,1,0:T(8,128)(2,1)S(1)}, u32[]{:S(2)}, u32[]{:S(2)}) async-start(bf16[64,16,128]{2,1,0:T(8,128)(2,1)} %add_rows.1), calls=%async_computation.3 | async-start | bytes 524288 | tf_op jit(solution)/shard_map/all_to_all | solution.py:332
  99.3 0.7 copy-start.1

commit v3 on v2

--- a/solution.py
+++ b/solution.py
@@ -11,7 +11,7 @@
 HD = 128
 PAD = 16
 NEG = -1e30
-VMEM = 60 * 1024 * 1024
+VMEM = 24 * 1024 * 1024
 
 
 def stack_heads(ref, out, part, rows, group, stride):
@@ -37,11 +37,6 @@
     row = lax.broadcasted_iota(jnp.int32, (rows, stride), 1)
     tile = jnp.where(jnp.logical_and(inside <= row, inside < length), 0.0, NEG)
     bias[...] = jnp.concatenate([tile] * group, axis=1)
-
-
-def prologue(q4, g4):
-    q4[...] = jnp.zeros_like(q4)
-    g4[...] = jnp.zeros_like(g4)
 
 
 def own_stats(dims, skips, where, index, lengths, prefixes, q, g, k, v, *refs):
@@ -55,9 +50,10 @@
         meta[1] = prefixes[index[where[1]]]
         for i, skip in enumerate(skips):
             members[i] = index[where[0] + skip]
-        prologue(q4, g4)
         own_bias(bias, length, rows, group, stride)
 
+    q4[...] = jnp.zeros_like(q4)
+    g4[...] = jnp.zeros_like(g4)
     for part in range(q4.shape[0]):
         stack_heads(q, q4, part, rows, group, stride)
         stack_heads(g, g4, part, rows, group, stride)
@@ -82,20 +78,14 @@
     return jnp.where(column < prefix_length, 0.0, NEG)
 
 
-def prefix_terms(dims, meta, q, g, stats, pair, total, terms, q4, g4):
+def prefix_terms(dims, meta, q4, g4, stats, pair, total, terms):
     rows, group, stride, factor, scale = dims
     half = pair.shape[0] // 2
     prefix_rows = half * pair.shape[2]
 
-    @pl.when(pl.program_id(0) == 0)
-    def _():
-        prologue(q4, g4)
-
     mask = prefix_bias(meta[1], prefix_rows, group * stride)
     live = live_lanes(meta[0], group, stride)
     for part in range(q4.shape[0]):
-        stack_heads(q, q4, part, rows, group, stride)
-        stack_heads(g, g4, part, rows, group, stride)
         keys = pair[0:half, part].reshape(prefix_rows, HD)
         values = pair[half:, part].reshape(prefix_rows, HD)
         scores = dot_nt(keys, q4[part]) * factor + mask
@@ -119,20 +109,17 @@
         terms[half:, part] = value_terms.astype(jnp.bfloat16).reshape((half,) + terms.shape[2:])
 
 
-def own_grads(dims, meta, q, g, k, v, total, pair, dq, dk, dv, q4, g4, bias):
+def own_grads(dims, meta, q4, g4, k, v, total, pair, dq, dk, dv, bias):
     rows, group, stride, factor, scale = dims
     half = pair.shape[0] // 2
     prefix_rows = half * pair.shape[2]
 
     @pl.when(pl.program_id(0) == 0)
     def _():
-        prologue(q4, g4)
         own_bias(bias, meta[0], rows, group, stride)
 
     prefix_mask = prefix_bias(meta[1], prefix_rows, group * stride)
     for part in range(q4.shape[0]):
-        stack_heads(q, q4, part, rows, group, stride)
-        stack_heads(g, g4, part, rows, group, stride)
         highest = total[part, 0:1, :]
         inverse = total[part, 1:2, :]
         delta = total[part, 2:3, :]
@@ -182,22 +169,11 @@
     out[...] = acc[...].astype(jnp.bfloat16)
 
 
-def sum_rows(places, source, keys, values):
-    piece = source.shape[1]
-    count = max(places) + 1
-    totals = [None] * count
-    for i, place in enumerate(places):
-        row = source[i].astype(jnp.float32)
-        totals[place] = row if totals[place] is None else totals[place] + row
-    for place, total in enumerate(totals):
-        out = keys if place < count // 2 else values
-        at = (place % (count // 2)) * piece
-        size = max(0, min(piece, out.shape[1] - at))
-        if size:
-            out[0, at : at + size, :] = total[:size]
-
-
 PARAMS = pltpu.CompilerParams(vmem_limit_bytes=VMEM)
+
+
+def streamed(*arrays):
+    return tuple(pltpu.with_memory_space_constraint(array, pltpu.HBM) for array in arrays)
 
 
 def cost(flops, nbytes):
@@ -255,7 +231,8 @@
     heads_k = pl.BlockSpec((1, rows, per * HD), lambda i: (0, 0, i))
     lanes = pl.BlockSpec((per, 8, width), lambda i: (i, 0, 0))
     parted = pl.BlockSpec((pieces, per, piece, HD), lambda i: (0, i, 0, 0))
-    packed = pltpu.VMEM((per, width, HD), jnp.bfloat16)
+    stacked = pl.BlockSpec((per, width, HD), lambda i: (i, 0, 0))
+    stacked_shape = jax.ShapeDtypeStruct((kv_heads, width, HD), jnp.bfloat16)
     bias = pltpu.VMEM((rows, width), jnp.float32)
     lane_shape = jax.ShapeDtypeStruct((kv_heads, 8, width), jnp.float32)
     far_shape = (n_far, piece, HD)
@@ -271,31 +248,35 @@
         scratch_shapes=[pltpu.VMEM((pieces * piece, HD), jnp.bfloat16)],
         compiler_params=PARAMS,
         name="spread",
-    )(prefix_keys, prefix_values)
+    )(*streamed(prefix_keys, prefix_values))
     held = lax.all_to_all(everyone, far, 0, 0, tiled=True)
-    meta, members, stats = pl.pallas_call(
+    meta, members, stats, stacked_queries, stacked_grads = pl.pallas_call(
         functools.partial(own_stats, dims, skips),
         grid=(steps,),
         in_specs=[smem, smem, smem, smem, heads_q, heads_q, heads_k, heads_k],
-        out_specs=[smem, smem, lanes],
-        scratch_shapes=[packed, packed, bias],
+        out_specs=[smem, smem, lanes, stacked, stacked],
+        scratch_shapes=[bias],
         out_shape=[
             jax.ShapeDtypeStruct((2,), jnp.int32),
             jax.ShapeDtypeStruct((n_near,), jnp.int32),
             lane_shape,
+            stacked_shape,
+            stacked_shape,
         ],
         compiler_params=PARAMS,
         cost_estimate=cost(2 * big, 3 << 20),
         name="own_stats",
     )(
         where,
-        query_index,
-        candidate_length,
-        prefix_length,
-        queries,
-        grad_output,
-        candidate_keys,
-        candidate_values,
+        *streamed(
+            query_index,
+            candidate_length,
+            prefix_length,
+            queries,
+            grad_output,
+            candidate_keys,
+            candidate_values,
+        ),
     )
     chosen = pl.pallas_call(
         pick_rows,
@@ -310,14 +291,13 @@
     total, terms = pl.pallas_call(
         functools.partial(prefix_terms, dims),
         grid=(steps,),
-        in_specs=[smem, heads_q, heads_q, lanes, parted],
+        in_specs=[smem, stacked, stacked, lanes, parted],
         out_specs=[lanes, parted],
-        scratch_shapes=[packed, packed],
         out_shape=[lane_shape, jax.ShapeDtypeStruct(part_shape, jnp.bfloat16)],
         compiler_params=PARAMS,
         cost_estimate=cost(2 * big, 3 << 20),
         name="prefix_terms",
-    )(meta, queries, grad_output, stats, pairs)
+    )(meta, stacked_queries, stacked_grads, stats, pairs)
 
     returned = lax.all_to_all(terms.reshape(near_shape), near, 0, 0, tiled=True)
     summed = pl.pallas_call(
@@ -330,21 +310,16 @@
         name="add_rows",
     )(members, returned)
     owned = lax.all_to_all(summed, far, 0, 0, tiled=True)
-    grad_prefix_keys, grad_prefix_values = pl.pallas_call(
-        functools.partial(sum_rows, places),
-        in_specs=[vmem],
-        out_specs=[vmem, vmem],
-        out_shape=[jax.ShapeDtypeStruct((1, prefix_rows, HD), jnp.float32)] * 2,
-        compiler_params=PARAMS,
-        name="sum_rows",
-    )(owned)
+    owned = owned.reshape(sizes + (piece, HD)).astype(jnp.float32)
+    owned = jnp.sum(owned, axis=(0, 2)).reshape(2, half * piece, HD)
+    grad_prefix_keys, grad_prefix_values = owned[0:1, :prefix_rows], owned[1:2, :prefix_rows]
 
     grad_queries, grad_keys, grad_values = pl.pallas_call(
         functools.partial(own_grads, dims),
         grid=(steps,),
-        in_specs=[smem, heads_q, heads_q, heads_k, heads_k, lanes, parted],
+        in_specs=[smem, stacked, stacked, heads_k, heads_k, lanes, parted],
         out_specs=[heads_q, heads_k, heads_k],
-        scratch_shapes=[packed, packed, bias],
+        scratch_shapes=[bias],
         out_shape=[
             jax.ShapeDtypeStruct(queries.shape, jnp.bfloat16),
             jax.ShapeDtypeStruct(candidate_keys.shape, jnp.bfloat16),
@@ -353,7 +328,7 @@
         compiler_params=PARAMS,
         cost_estimate=cost(6 * big, 6 << 20),
         name="own_grads",
-    )(meta, queries, grad_output, candidate_keys, candidate_values, total, pairs)
+    )(meta, stacked_queries, stacked_grads, candidate_keys, candidate_values, total, pairs)
     return grad_queries, grad_keys, grad_values, grad_prefix_keys, grad_prefix_values
 
 

time: 102 us -> 97.8 us (0.959)
  Pallas kernels: 25.8 us -> 20.4 us
    pallas_call x1, Pallas kernels: 5.55 us -> 3.93 us  [local(): pl.pallas_call(functools.partial(prefix_terms, dims), grid=(steps,), in_s...]
    pallas_call x1 -> x0, Pallas kernels: 1.59 us -> none  [local(): pl.pallas_call(functools.partial(sum_rows, places), in_specs=[vmem], out_...]
    pallas_call x1, Pallas kernels: 1.71 us -> 0.59 us  [local(): pl.pallas_call(pick_rows, in_specs=[smem, vmem], out_specs=vmem, out_shap...]
  transfers between devices with their start and end apart: 2 -> 2, of which waited for: 2 -> 2; matrix products, arithmetic and copies ran while one was open for 1% -> 0% of each run, Pallas kernels for 13% -> 13%
where the time goes in v3:
time: 97.8 us; the launch traced here: 97.3 us
  blocking collectives  34.2 us (35%)
  starting transfers between devices  23.7 us (24%)
  Pallas kernels  20.4 us (21%)
  waiting for transfers between devices  15 us (15%)
  local copies, waits for them, and re-layouts  2.2 us (2%)
  other arithmetic  1.07 us (1%)
    all_to_all x1, blocking collectives, local(): pairs = lax.all_to_all(chosen, near, 0, 0, tiled=True).reshape(part_shape)  17.7 us
    all_to_all x1, starting transfers between devices, local(): held = lax.all_to_all(everyone, far, 0, 0, tiled=True)  16.6 us
    all_to_all x1, blocking collectives, local(): returned = lax.all_to_all(terms.reshape(near_shape), near, 0, 0, tiled=True)  16.5 us
    all_to_all x1, waiting for transfers between devices, local(): held = lax.all_to_all(everyone, far, 0, 0, tiled=True)  9.51 us
    pallas_call x1, Pallas kernels, local(): pl.pallas_call(functools.partial(own_grads, dims), grid=(steps,), in_spec...  8.11 us
    all_to_all x1, starting transfers between devices, local(): owned = lax.all_to_all(summed, far, 0, 0, tiled=True)  7.13 us
    all_to_all x1, waiting for transfers between devices, local(): owned = lax.all_to_all(summed, far, 0, 0, tiled=True)  5.46 us
    pallas_call x1, Pallas kernels, local(): pl.pallas_call(functools.partial(own_stats, dims, skips), grid=(steps,),...  4.72 us
  transfers between devices with their start and end apart: 2, of which 2 were waited for; matrix products, arithmetic and copies ran while one was open for 0% of the time, Pallas kernels for 13%

profile of v3, /device:TPU:8, one launch (start us, length us, event | category | flops | bytes accessed | tf_op | source)
XLA Modules:
  0.0 97.3 jit_solution(10469932615589787719)
XLA Ops:
  0.6 1.5 %spread.1 = bf16[64,16,128]{2,1,0:T(8,128)(2,1)} custom-call(bf16[1,56,128]{2,1,0:T(8,128)(2,1)} %keys.1, bf16[1,56,128]{2,1,0:T(8,128)(2,1)} %values.1), custom_call_target="tpu_custom_call" | custom-call | tf_op jit(solution)/shard_map/spread/pallas_call | solution.py:243
  2.1 16.6 %all-to-all-start = ((bf16[64,16,128]{2,1,0:T(8,128)(2,1)}), bf16[64,16,128]{2,1,0:T(8,128)(2,1)S(1)}, u32[]{:S(2)}, u32[]{:S(2)}) async-start(bf16[64,16,128]{2,1,0:T(8,128)(2,1)} %spread.1), calls=%async_computation | async-start | bytes 524288 | tf_op jit(solution)/shard_map/all_to_all | solution.py:252
  18.7 0.1 pad_add_fusion.where
  18.8 4.7 %own_stats.1 = (s32[2]{0:T(128)S(1)}, s32[64]{0:T(128)S(1)}, f32[8,8,640]{2,1,0:T(8,128)S(1)}, bf16[8,640,128]{2,1,0:T(8,128)(2,1)S(1)}, bf16[8,640,128]{2,1,0:T(8,128)(2,1)S(1)}) custom-call(s32[2]{0:T(128)S(1)} %pad_add_fusion.where, s32[512]{0:T(512)} %index.1, s32[512]{0:T(512)} %lengths.1, s32[64]{0:T(128)} %prefixes.1, bf16[1,152,4096]{2,1,0:T(8,128)(2,1)} %q.1, ...), custom_call_target="tpu_custom_call" | custom-call | flops 398458880 | bytes 3145728 | tf_op jit(solution)/shard_map/own_stats/pallas_call | solution.py:253
  23.5 9.5 %all-to-all-done.source = bf16[64,16,128]{2,1,0:T(8,128)(2,1)S(1)} async-done(((bf16[64,16,128]{2,1,0:T(8,128)(2,1)}), bf16[64,16,128]{2,1,0:T(8,128)(2,1)S(1)}, u32[]{:S(2)}, u32[]{:S(2)}) %all-to-all-start) | async-done | bytes 262176 | tf_op jit(solution)/shard_map/all_to_all | solution.py:252
  33.0 0.6 pick_rows.1
  33.6 17.7 %all_to_all.20 = bf16[64,16,128]{2,1,0:T(8,128)(2,1)S(1)} all-to-all(bf16[64,16,128]{2,1,0:T(8,128)(2,1)S(1)} %pick_rows.1), channel_id=1, replica_groups=mesh['zh'=4,'zl'=2,'yh'=2,'yl'=4,'seq'=8] {'zl','yl','seq'}, dimensions={0} | all-to-all | bytes 524288 | tf_op jit(solution)/shard_map/all_to_all | solution.py:289
  51.3 3.9 %prefix_terms.1 = (f32[8,8,640]{2,1,0:T(8,128)S(1)}, bf16[8,8,16,128]{3,2,1,0:T(8,128)(2,1)S(1)}) custom-call(s32[2]{0:T(128)S(1)} %get-tuple-element.15.meta, bf16[8,640,128]{2,1,0:T(8,128)(2,1)S(1)} %get-tuple-element.16.q4, bf16[8,640,128]{2,1,0:T(8,128)(2,1)S(1)} %get-tuple-element.17.g4, f32[8,8,640]{2,1,0:T(8,128)S(1)} %get-tuple-element.18.stats, ...), custom_call_target="tpu_custom_call" | custom-call | flops 398458880 | bytes 3145728 | tf_op jit(solution)/shard_map/prefix_terms/pallas_call | solution.py:291
  55.3 0.0 copy-start.2
  55.3 0.7 copy-done.2
  55.9 0.0 copy-start
  55.9 0.0 copy-start.1
  55.9 16.5 %all_to_all.21.source = bf16[64,16,128]{2,1,0:T(8,128)(2,1)S(1)} all-to-all(bf16[64,16,128]{2,1,0:T(8,128)(2,1)S(1)} %bitcast.9), channel_id=1, replica_groups=mesh['zh'=4,'zl'=2,'yh'=2,'yl'=4,'seq'=8] {'zl','yl','seq'}, dimensions={0} | all-to-all | bytes 524288 | tf_op jit(solution)/shard_map/all_to_all | solution.py:302
  72.4 1.6 %add_rows.1 = bf16[64,16,128]{2,1,0:T(8,128)(2,1)} custom-call(s32[64]{0:T(128)S(1)} %get-tuple-element.19.members, bf16[64,16,128]{2,1,0:T(8,128)(2,1)S(1)} %all_to_all.21.source), custom_call_target="tpu_custom_call" | custom-call | tf_op jit(solution)/shard_map/add_rows/pallas_call | solution.py:303
  74.0 7.1 %all-to-all-start.3 = ((bf16[64,16,128]{2,1,0:T(8,128)(2,1)}), bf16[64,16,128]{2,1,0:T(8,128)(2,1)}, u32[]{:S(2)}, u32[]{:S(2)}) async-start(bf16[64,16,128]{2,1,0:T(8,128)(2,1)} %add_rows.1), calls=%async_computation.3 | async-start | bytes 524288 | tf_op jit(solution)/shard_map/all_to_all | solution.py:312
  81.2 0.0 copy-done
  81.2 0.0 copy-done.1
  81.2 0.0 copy-start.3
  81.2 0.9 copy-done.3
  82.1 8.1 %own_grads.1 = (bf16[1,152,4096]{2,1,0:T(8,128)(2,1)}, bf16[1,152,1024]{2,1,0:T(8,128)(2,1)}, bf16[1,152,1024]{2,1,0:T(8,128)(2,1)}) custom-call(s32[2]{0:T(128)S(1)} %get-tuple-element.15.meta, bf16[8,640,128]{2,1,0:T(8,128)(2,1)S(1)} %get-tuple-element.16.q4, bf16[8,640,128]{2,1,0:T(8,128)(2,1)S(1)} %get-tuple-element.17.g4, ...), custom_call_target="tpu_custom_call" | custom-call | flops 1195376640 | bytes 6291456 | tf_op jit(solution)/shard_map/own_grads/pallas_call | solution.py:317
  90.2 5.5 %all-to-all-done.3 = bf16[64,16,128]{2,1,0:T(8,128)(2,1)} async-done(((bf16[64,16,128]{2,1,0:T(8,128)(2,1)}), bf16[64,16,128]{2,1,0:T(8,128)(2,1)}, u32[]{:S(2)}, u32[]{:S(2)}) %all-to-all-start.3) | async-done | bytes 262176 | tf_op jit(solution)/shard_map/all_to_all | solution.py:312
  95.7 1.0 %convert_reduce_fusion = f32[2,4,16,128]{3,2,1,0:T(8,128)S(1)} fusion(bf16[4,2,2,4,16,128]{5,4,3,2,1,0:T(8,128)(2,1)} %bitcast.6), kind=kLoop, calls=%fused_computation | loop fusion | flops 245760 | bytes 327680 | tf_op jit(solution)/shard_map/reduce_sum | solution.py:314
  96.7 0.6 fusion
Async XLA Ops:
  2.1 30.9 %all-to-all-start = ((bf16[64,16,128]{2,1,0:T(8,128)(2,1)}), bf16[64,16,128]{2,1,0:T(8,128)(2,1)S(1)}, u32[]{:S(2)}, u32[]{:S(2)}) async-start(bf16[64,16,128]{2,1,0:T(8,128)(2,1)} %spread.1), calls=%async_computation | async-start | bytes 524288 | tf_op jit(solution)/shard_map/all_to_all | solution.py:252
  55.3 0.7 copy-start.2
  55.9 25.2 %copy-start = (bf16[1,152,1024]{2,1,0:T(8,128)(2,1)S(1)}, bf16[1,152,1024]{2,1,0:T(8,128)(2,1)}, u32[]{:S(2)}) copy-start(bf16[1,152,1024]{2,1,0:T(8,128)(2,1)} %k.3) | copy-start | bytes 933892
  55.9 25.3 %copy-start.1 = (bf16[1,152,1024]{2,1,0:T(8,128)(2,1)S(1)}, bf16[1,152,1024]{2,1,0:T(8,128)(2,1)}, u32[]{:S(2)}) copy-start(bf16[1,152,1024]{2,1,0:T(8,128)(2,1)} %v.3) | copy-start | bytes 933892
  74.0 21.7 %all-to-all-start.3 = ((bf16[64,16,128]{2,1,0:T(8,128)(2,1)}), bf16[64,16,128]{2,1,0:T(8,128)(2,1)}, u32[]{:S(2)}, u32[]{:S(2)}) async-start(bf16[64,16,128]{2,1,0:T(8,128)(2,1)} %add_rows.1), calls=%async_computation.3 | async-start | bytes 524288 | tf_op jit(solution)/shard_map/all_to_all | solution.py:312
  81.2 0.9 copy-start.3

commit v4 on v3

--- a/solution.py
+++ b/solution.py
@@ -290,9 +290,8 @@
 
     total, terms = pl.pallas_call(
         functools.partial(prefix_terms, dims),
-        grid=(steps,),
-        in_specs=[smem, stacked, stacked, lanes, parted],
-        out_specs=[lanes, parted],
+        in_specs=[smem, vmem, vmem, vmem, vmem],
+        out_specs=[vmem, vmem],
         out_shape=[lane_shape, jax.ShapeDtypeStruct(part_shape, jnp.bfloat16)],
         compiler_params=PARAMS,
         cost_estimate=cost(2 * big, 3 << 20),
@@ -328,7 +327,14 @@
         compiler_params=PARAMS,
         cost_estimate=cost(6 * big, 6 << 20),
         name="own_grads",
-    )(meta, stacked_queries, stacked_grads, candidate_keys, candidate_values, total, pairs)
+    )(
+        meta,
+        stacked_queries,
+        stacked_grads,
+        *streamed(candidate_keys, candidate_values),
+        total,
+        pairs,
+    )
     return grad_queries, grad_keys, grad_values, grad_prefix_keys, grad_prefix_values
 
 

time: 97.8 us -> 95.5 us (0.976)
  local copies, waits for them, and re-layouts: 2.2 us -> 0.62 us
    unnamed x8 -> x0, local copies, waits for them, and re-layouts: 1.58 us -> none
  transfers between devices with their start and end apart: 2 -> 2, of which waited for: 2 -> 2; matrix products, arithmetic and copies ran while one was open for 0% -> 0% of each run, Pallas kernels for 13% -> 14%
where the time goes in v4:
time: 95.5 us; the launch traced here: 95 us
  blocking collectives  34.1 us (36%)
  starting transfers between devices  23.5 us (25%)
  Pallas kernels  20.3 us (21%)
  waiting for transfers between devices  15.6 us (16%)
    all_to_all x1, blocking collectives, local(): pairs = lax.all_to_all(chosen, near, 0, 0, tiled=True).reshape(part_shape)  17.7 us
    all_to_all x1, starting transfers between devices, local(): held = lax.all_to_all(everyone, far, 0, 0, tiled=True)  16.6 us
    all_to_all x1, blocking collectives, local(): returned = lax.all_to_all(terms.reshape(near_shape), near, 0, 0, tiled=True)  16.4 us
    all_to_all x1, waiting for transfers between devices, local(): held = lax.all_to_all(everyone, far, 0, 0, tiled=True)  9.51 us
    pallas_call x1, Pallas kernels, local(): pl.pallas_call(functools.partial(own_grads, dims), grid=(steps,), in_spec...  8.46 us
    all_to_all x1, starting transfers between devices, local(): owned = lax.all_to_all(summed, far, 0, 0, tiled=True)  6.95 us
    all_to_all x1, waiting for transfers between devices, local(): owned = lax.all_to_all(summed, far, 0, 0, tiled=True)  6.14 us
    pallas_call x1, Pallas kernels, local(): pl.pallas_call(functools.partial(own_stats, dims, skips), grid=(steps,),...  4.72 us
  transfers between devices with their start and end apart: 2, of which 2 were waited for; matrix products, arithmetic and copies ran while one was open for 0% of the time, Pallas kernels for 14%

profile of v4, /device:TPU:8, one launch (start us, length us, event | category | flops | bytes accessed | tf_op | source)
XLA Modules:
  0.0 95.0 jit_solution(16418394514046443237)
XLA Ops:
  0.6 1.5 %spread.1 = bf16[64,16,128]{2,1,0:T(8,128)(2,1)} custom-call(bf16[1,56,128]{2,1,0:T(8,128)(2,1)} %keys.1, bf16[1,56,128]{2,1,0:T(8,128)(2,1)} %values.1), custom_call_target="tpu_custom_call" | custom-call | tf_op jit(solution)/shard_map/spread/pallas_call | solution.py:243
  2.1 16.6 %all-to-all-start = ((bf16[64,16,128]{2,1,0:T(8,128)(2,1)}), bf16[64,16,128]{2,1,0:T(8,128)(2,1)S(1)}, u32[]{:S(2)}, u32[]{:S(2)}) async-start(bf16[64,16,128]{2,1,0:T(8,128)(2,1)} %spread.1), calls=%async_computation | async-start | bytes 524288 | tf_op jit(solution)/shard_map/all_to_all | solution.py:252
  18.7 0.1 pad_add_fusion.where
  18.8 4.7 %own_stats.1 = (s32[2]{0:T(128)S(1)}, s32[64]{0:T(128)S(1)}, f32[8,8,640]{2,1,0:T(8,128)S(1)}, bf16[8,640,128]{2,1,0:T(8,128)(2,1)S(1)}, bf16[8,640,128]{2,1,0:T(8,128)(2,1)S(1)}) custom-call(s32[2]{0:T(128)S(1)} %pad_add_fusion.where, s32[512]{0:T(512)} %index.1, s32[512]{0:T(512)} %lengths.1, s32[64]{0:T(128)} %prefixes.1, bf16[1,152,4096]{2,1,0:T(8,128)(2,1)} %q.1, ...), custom_call_target="tpu_custom_call" | custom-call | flops 398458880 | bytes 3145728 | tf_op jit(solution)/shard_map/own_stats/pallas_call | solution.py:253
  23.5 9.5 %all-to-all-done.source = bf16[64,16,128]{2,1,0:T(8,128)(2,1)S(1)} async-done(((bf16[64,16,128]{2,1,0:T(8,128)(2,1)}), bf16[64,16,128]{2,1,0:T(8,128)(2,1)S(1)}, u32[]{:S(2)}, u32[]{:S(2)}) %all-to-all-start) | async-done | bytes 262176 | tf_op jit(solution)/shard_map/all_to_all | solution.py:252
  33.0 0.6 pick_rows.1
  33.6 17.7 %all_to_all.20 = bf16[64,16,128]{2,1,0:T(8,128)(2,1)S(1)} all-to-all(bf16[64,16,128]{2,1,0:T(8,128)(2,1)S(1)} %pick_rows.1), channel_id=1, replica_groups=mesh['zh'=4,'zl'=2,'yh'=2,'yl'=4,'seq'=8] {'zl','yl','seq'}, dimensions={0} | all-to-all | bytes 524288 | tf_op jit(solution)/shard_map/all_to_all | solution.py:289
  51.3 3.5 %prefix_terms.1 = (f32[8,8,640]{2,1,0:T(8,128)S(1)}, bf16[8,8,16,128]{3,2,1,0:T(8,128)(2,1)S(1)}) custom-call(s32[2]{0:T(128)S(1)} %get-tuple-element.15.meta, bf16[8,640,128]{2,1,0:T(8,128)(2,1)S(1)} %get-tuple-element.16.q4, bf16[8,640,128]{2,1,0:T(8,128)(2,1)S(1)} %get-tuple-element.17.g4, f32[8,8,640]{2,1,0:T(8,128)S(1)} %get-tuple-element.18.stats, ...), custom_call_target="tpu_custom_call" | custom-call | flops 398458880 | bytes 3145728 | tf_op jit(solution)/shard_map/prefix_terms/pallas_call | solution.py:291
  54.8 16.4 %all_to_all.21.source = bf16[64,16,128]{2,1,0:T(8,128)(2,1)S(1)} all-to-all(bf16[64,16,128]{2,1,0:T(8,128)(2,1)S(1)} %bitcast.9), channel_id=1, replica_groups=mesh['zh'=4,'zl'=2,'yh'=2,'yl'=4,'seq'=8] {'zl','yl','seq'}, dimensions={0} | all-to-all | bytes 524288 | tf_op jit(solution)/shard_map/all_to_all | solution.py:301
  71.2 1.6 %add_rows.1 = bf16[64,16,128]{2,1,0:T(8,128)(2,1)} custom-call(s32[64]{0:T(128)S(1)} %get-tuple-element.19.members, bf16[64,16,128]{2,1,0:T(8,128)(2,1)S(1)} %all_to_all.21.source), custom_call_target="tpu_custom_call" | custom-call | tf_op jit(solution)/shard_map/add_rows/pallas_call | solution.py:302
  72.8 6.9 %all-to-all-start.3 = ((bf16[64,16,128]{2,1,0:T(8,128)(2,1)}), bf16[64,16,128]{2,1,0:T(8,128)(2,1)S(1)}, u32[]{:S(2)}, u32[]{:S(2)}) async-start(bf16[64,16,128]{2,1,0:T(8,128)(2,1)} %add_rows.1), calls=%async_computation.3 | async-start | bytes 524288 | tf_op jit(solution)/shard_map/all_to_all | solution.py:311
  79.7 8.5 %own_grads.1 = (bf16[1,152,4096]{2,1,0:T(8,128)(2,1)}, bf16[1,152,1024]{2,1,0:T(8,128)(2,1)}, bf16[1,152,1024]{2,1,0:T(8,128)(2,1)}) custom-call(s32[2]{0:T(128)S(1)} %get-tuple-element.15.meta, bf16[8,640,128]{2,1,0:T(8,128)(2,1)S(1)} %get-tuple-element.16.q4, bf16[8,640,128]{2,1,0:T(8,128)(2,1)S(1)} %get-tuple-element.17.g4, bf16[1,152,1024]{2,1,0:T(8,128)(2,1)} %k.3, ...), custom_call_target="tpu_custom_call" | custom-call | flops 1195376640 | bytes 6291456 | tf_op jit(solution)/shard_map/own_grads/pallas_call | solution.py:316
  88.2 6.1 %all-to-all-done.3 = bf16[64,16,128]{2,1,0:T(8,128)(2,1)S(1)} async-done(((bf16[64,16,128]{2,1,0:T(8,128)(2,1)}), bf16[64,16,128]{2,1,0:T(8,128)(2,1)S(1)}, u32[]{:S(2)}, u32[]{:S(2)}) %all-to-all-start.3) | async-done | bytes 262176 | tf_op jit(solution)/shard_map/all_to_all | solution.py:311
  94.3 0.6 fusion
  (1 shorter events, 0.0 us)
Async XLA Ops:
  2.1 30.9 %all-to-all-start = ((bf16[64,16,128]{2,1,0:T(8,128)(2,1)}), bf16[64,16,128]{2,1,0:T(8,128)(2,1)S(1)}, u32[]{:S(2)}, u32[]{:S(2)}) async-start(bf16[64,16,128]{2,1,0:T(8,128)(2,1)} %spread.1), calls=%async_computation | async-start | bytes 524288 | tf_op jit(solution)/shard_map/all_to_all | solution.py:252
  72.8 21.6 %all-to-all-start.3 = ((bf16[64,16,128]{2,1,0:T(8,128)(2,1)}), bf16[64,16,128]{2,1,0:T(8,128)(2,1)S(1)}, u32[]{:S(2)}, u32[]{:S(2)}) async-start(bf16[64,16,128]{2,1,0:T(8,128)(2,1)} %add_rows.1), calls=%async_computation.3 | async-start | bytes 524288 | tf_op jit(solution)/shard_map/all_to_all | solution.py:311
